TPU v7x, 32 devices: a whole 2x2x4 slice. The times are simulated.
32 devices in a mesh: call: 2 (over x), tm: 16 (over z, y, core).
Axes of the slice: x: 2, y: 2, z: 4, core: 2. Of those that a mesh axis runs over, the one named last changes fastest.
Arguments:
- frames: bfloat16 [2, 2048, 1024], P('call', 'tm'), may hold values from -6 to 6
- lengths: int32 [2], replicated, may hold values from 512 to 2048, as said below
- ln_attn_gain: float32 [1024], replicated, may hold values from 0.5 to 1.5
- w_qkv: bfloat16 [1024, 3072], P('tm'), may hold values from -0.1875 to 0.1875
- w_out: bfloat16 [1024, 1024], P('tm'), may hold values from -1.5 to 1.5
- ln_conv_gain: float32 [1024], replicated, may hold values from 0.5 to 1.5
- w_pw1: bfloat16 [1024, 2048], P('tm'), may hold values from -0.1875 to 0.1875
- dw_kernel: float32 [9, 1024], replicated, may hold values from -2 to 2
- bn_gain: float32 [1024], replicated, may hold values from 0.5 to 1.5
- bn_bias: float32 [1024], replicated, may hold values from -3 to 3
Outputs:
- attended: bfloat16 [2, 2048, 1024], P('call', 'tm')
- conv_act: bfloat16 [2, 2048, 1024], P('call', 'tm')
Inputs may be any that keep to these rules, and one draw needn't show every extreme that they name: `lengths`: valid frames of each call; at least one call of the batch fills all 2048 frames.
All inputs are finite; a program needn't handle non-finite values.
Results may differ from a plain program's by a relative error of at most 0.009.
Values may be sent and summed in bfloat16 or wider, within the bound.
A program may use at most 64 MiB of HBM per device.

v0:
```python
import jax
import jax.numpy as jnp
from jax import lax
from jax.sharding import PartitionSpec as P

HEAD_DIM = 64
SPAN = 128
LEFT = 1024
KERNEL = 9


def passed_along(value, axis, steps):
    count = lax.axis_size(axis)
    first, last = (max(0, -steps), min(count, count - steps))
    return lax.ppermute(value, axis, [(source, source + steps) for source in range(first, last)])


def with_halo(cells, sides, width):
    for axis, dim in sides:
        count = lax.axis_size(axis)
        ends = count - 1
        head = lax.slice_in_dim(cells, 0, width, axis=dim)
        tail = lax.slice_in_dim(cells, cells.shape[dim] - width, cells.shape[dim], axis=dim)
        cells = jnp.concatenate(
            [
                lax.ppermute(tail, axis, [(i, (i + 1) % count) for i in range(ends)]),
                cells,
                lax.ppermute(head, axis, [((i + 1) % count, i) for i in range(ends)]),
            ],
            axis=dim,
        )
    return cells


def layer_norm(values, gain_vec):
    wide = values.astype(jnp.float32)
    center = wide - jnp.mean(wide, axis=-1, keepdims=True)
    spread = jnp.mean(center * center, axis=-1, keepdims=True)
    return center * lax.rsqrt(spread + 1e-05) * gain_vec


def contract_with(left, rows_piece):
    return jnp.dot(left, rows_piece, preferred_element_type=jnp.float32)


def on_device(
    frames, lengths, ln_attn_gain, w_qkv, w_out, ln_conv_gain, w_pw1, dw_kernel, bn_gain, bn_bias
):
    stream = frames[0]
    frame_count, model_width = stream.shape
    head_count = model_width // HEAD_DIM
    length = lax.dynamic_index_in_dim(lengths, lax.axis_index("call"), 0, keepdims=False)
    first_row = lax.axis_index("tm") * frame_count
    query_pos = first_row + jnp.arange(frame_count, dtype=jnp.int32)
    frame_valid = query_pos < length
    normed = layer_norm(stream, ln_attn_gain).astype(jnp.bfloat16)
    prior_blocks = LEFT // frame_count
    packed = contract_with(normed, lax.all_gather(w_qkv, "tm", axis=0, tiled=True))
    queries = packed[:, :model_width].astype(jnp.bfloat16)
    key_value = jnp.stack(
        [
            packed[:, model_width : 2 * model_width].astype(jnp.bfloat16),
            packed[:, 2 * model_width :].astype(jnp.bfloat16),
        ]
    )
    blocks = []
    current = key_value
    for hop_index in range(prior_blocks):
        current = passed_along(current, "tm", 1)
        blocks.append(current)
    context_kv = jnp.concatenate(blocks[::-1] + [key_value], axis=1)
    key_count = context_kv.shape[1]
    key_pos = first_row - prior_blocks * frame_count + jnp.arange(key_count, dtype=jnp.int32)
    span_first = query_pos // SPAN * SPAN
    allowed = (key_pos[None, :] >= 0) & (key_pos[None, :] >= span_first[:, None] - LEFT)
    allowed = allowed & (key_pos[None, :] < span_first[:, None] + SPAN)
    allowed = allowed & ((key_pos[None, :] < length) | (key_pos[None, :] == query_pos[:, None]))
    group_size = 4
    group_count = head_count // group_size
    query_groups = queries.reshape(frame_count, group_count, group_size, HEAD_DIM).transpose(
        1, 0, 2, 3
    )
    key_groups = (
        context_kv[0].reshape(key_count, group_count, group_size, HEAD_DIM).transpose(1, 0, 2, 3)
    )
    value_groups = (
        context_kv[1].reshape(key_count, group_count, group_size, HEAD_DIM).transpose(1, 0, 2, 3)
    )
    scale_factor = 1.0 / jnp.sqrt(jnp.float32(HEAD_DIM))

    def attend_group(operands):
        query_part, key_part, value_part = operands
        scores = (
            jnp.einsum("qhd,khd->hqk", query_part, key_part, preferred_element_type=jnp.float32)
            * scale_factor
        )
        raised = jnp.where(allowed[None], jnp.exp(scores), 0.0)
        probs = (raised / jnp.sum(raised, axis=-1, keepdims=True)).astype(jnp.bfloat16)
        mixed = jnp.einsum("hqk,khd->qhd", probs, value_part, preferred_element_type=jnp.float32)
        return mixed.astype(jnp.bfloat16)

    context = lax.map(attend_group, (query_groups, key_groups, value_groups))
    context = context.transpose(1, 0, 2, 3).reshape(frame_count, model_width)
    projected = contract_with(context, lax.all_gather(w_out, "tm", axis=0, tiled=True))
    attended = jnp.where(frame_valid[:, None], stream.astype(jnp.float32) + projected, 0.0).astype(
        jnp.bfloat16
    )
    conv_in = layer_norm(attended, ln_conv_gain).astype(jnp.bfloat16)
    expanded = contract_with(conv_in, lax.all_gather(w_pw1, "tm", axis=0, tiled=True))
    gated = expanded[:, :model_width] * jax.nn.sigmoid(expanded[:, model_width:])
    gated = jnp.where(frame_valid[:, None], gated, 0.0).astype(jnp.bfloat16)
    padded = with_halo(gated, (("tm", 0),), KERNEL // 2)
    depthwise = jnp.zeros((frame_count, model_width), jnp.float32)
    for tap_index in range(KERNEL):
        depthwise = (
            depthwise
            + padded[tap_index : tap_index + frame_count].astype(jnp.float32) * dw_kernel[tap_index]
        )
    masked = jnp.where(frame_valid[:, None], depthwise, 0.0)
    first_moment, second_moment = lax.psum(
        (jnp.sum(masked, axis=0), jnp.sum(masked * depthwise, axis=0)), ("call", "tm")
    )
    count_all = jnp.sum(lengths).astype(jnp.float32)
    average = first_moment / count_all
    second = second_moment / count_all
    normal_act = (depthwise - average) * lax.rsqrt(
        second - average * average + 1e-05
    ) * bn_gain + bn_bias
    activated = normal_act * jax.nn.sigmoid(normal_act)
    conv_act = jnp.where(frame_valid[:, None], activated, 0.0).astype(jnp.bfloat16)
    return (attended[None], conv_act[None])


def solution(mesh):
    return jax.shard_map(
        on_device,
        mesh=mesh,
        in_specs=(
            P("call", "tm", None),
            P(),
            P(),
            P("tm", None),
            P("tm", None),
            P(),
            P("tm", None),
            P(),
            P(),
            P(),
        ),
        out_specs=(P("call", "tm", None), P("call", "tm", None)),
        check_vma=False,
    )
```

profile of v0, /device:TPU:0, one launch (start us, length us, event | category | flops | bytes accessed | tf_op | source)
XLA Modules:
  0.0 288.4 jit_solution(1018205197759743333)
XLA Ops:
  7.2 0.7 all-gather.4.cloned.1.call-update
  7.9 0.7 all-gather.6.cloned.1.call-update
  8.7 1.1 convert_reduce_fusion.1
  9.8 1.2 fusion.28
  11.0 63.9 %all-gather.4.cloned.1.call-done = bf16[1024,3072]{1,0:T(8,128)(2,1)} async-done(((bf16[64,3072]{1,0:T(8,128)(2,1)}), bf16[1024,3072]{1,0:T(8,128)(2,1)}) %all-gather.4.cloned.1.call-update) | async-done | bytes 6291472 | tf_op jit(solution)/shard_map/all_gather | solution.py:58
  74.9 4.0 %convolution_convert_fusion = bf16[128,3072]{1,0:T(8,128)(2,1)S(1)} fusion(bf16[1024,3072]{1,0:T(8,128)(2,1)} %all-gather.4.cloned.1.call-done, bf16[1,128,1024]{2,1,0:T(8,128)(2,1)} %param.12, f32[1024]{0:T(1024)} %param.14, f32[128]{0:T(128)S(1)} %add_rsqrt_fusion.2, f32[128]{0:T(128)S(1)} %broadcast_multiply_fusion.1), kind=kOutput, calls=%fused_computation.20 | convolution fusion | flops 806354944 | bytes 7345152 | tf_op jit(solution)/shard_map/dot_general | solution.py:43
  79.0 2.2 collective-permute-start
  81.2 1.5 collective-permute-done
  82.6 8.3 %collective-permute-start.1 = (bf16[2,128,1024]{2,1,0:T(8,128)(2,1)S(1)}, bf16[2,128,1024]{2,1,0:T(8,128)(2,1)S(1)}, u32[]{:S(2)}, u32[]{:S(2)}) collective-permute-start(bf16[2,128,1024]{2,1,0:T(8,128)(2,1)S(1)} %collective-permute-done), channel_id=1, source_target_pairs={{0,1},{1,2},{2,3},{3,4},{4,5},{5,6},{6,7},{7,8},{8,9},{9,10},{10,1... | collective-permute-start | bytes 1572872 | tf_op jit(solution)/shard_map/ppermute | solution.py:15
  91.0 1.5 collective-permute-done.1
  92.5 9.0 %collective-permute-start.2 = (bf16[2,128,1024]{2,1,0:T(8,128)(2,1)S(1)}, bf16[2,128,1024]{2,1,0:T(8,128)(2,1)S(1)}, u32[]{:S(2)}, u32[]{:S(2)}) collective-permute-start(bf16[2,128,1024]{2,1,0:T(8,128)(2,1)S(1)} %collective-permute-done.1), channel_id=1, source_target_pairs={{0,1},{1,2},{2,3},{3,4},{4,5},{5,6},{6,7},{7,8},{8,9},{9,10},{10,1... | collective-permute-start | bytes 1572872 | tf_op jit(solution)/shard_map/ppermute | solution.py:15
  101.5 1.5 collective-permute-done.2
  103.0 11.2 %collective-permute-start.3 = (bf16[2,128,1024]{2,1,0:T(8,128)(2,1)S(1)}, bf16[2,128,1024]{2,1,0:T(8,128)(2,1)S(1)}, u32[]{:S(2)}, u32[]{:S(2)}) collective-permute-start(bf16[2,128,1024]{2,1,0:T(8,128)(2,1)S(1)} %collective-permute-done.2), channel_id=1, source_target_pairs={{0,1},{1,2},{2,3},{3,4},{4,5},{5,6},{6,7},{7,8},{8,9},{9,10},{10,1... | collective-permute-start | bytes 1572872 | tf_op jit(solution)/shard_map/ppermute | solution.py:15
  114.2 1.5 collective-permute-done.3
  115.6 9.0 %collective-permute-start.4 = (bf16[2,128,1024]{2,1,0:T(8,128)(2,1)S(1)}, bf16[2,128,1024]{2,1,0:T(8,128)(2,1)S(1)}, u32[]{:S(2)}, u32[]{:S(2)}) collective-permute-start(bf16[2,128,1024]{2,1,0:T(8,128)(2,1)S(1)} %collective-permute-done.3), channel_id=1, source_target_pairs={{0,1},{1,2},{2,3},{3,4},{4,5},{5,6},{6,7},{7,8},{8,9},{9,10},{10,1... | collective-permute-start | bytes 1572872 | tf_op jit(solution)/shard_map/ppermute | solution.py:15
  124.7 1.5 collective-permute-done.4
  126.1 9.8 %collective-permute-start.5 = (bf16[2,128,1024]{2,1,0:T(8,128)(2,1)S(1)}, bf16[2,128,1024]{2,1,0:T(8,128)(2,1)}, u32[]{:S(2)}, u32[]{:S(2)}) collective-permute-start(bf16[2,128,1024]{2,1,0:T(8,128)(2,1)S(1)} %collective-permute-done.4), channel_id=1, source_target_pairs={{0,1},{1,2},{2,3},{3,4},{4,5},{5,6},{6,7},{7,8},{8,9},{9,10},{10,1... | collective-permute-start | bytes 1572872 | tf_op jit(solution)/shard_map/ppermute | solution.py:15
  135.9 0.8 collective-permute-done.5
  136.8 9.7 %collective-permute-start.6 = (bf16[2,128,1024]{2,1,0:T(8,128)(2,1)}, bf16[2,128,1024]{2,1,0:T(8,128)(2,1)}, u32[]{:S(2)}, u32[]{:S(2)}) collective-permute-start(bf16[2,128,1024]{2,1,0:T(8,128)(2,1)} %collective-permute-done.5), channel_id=1, source_target_pairs={{0,1},{1,2},{2,3},{3,4},{4,5},{5,6},{6,7},{7,8},{8,9},{9,10},{10,1... | collective-permute-start | bytes 1572872 | tf_op jit(solution)/shard_map/ppermute | solution.py:15
  146.4 0.6 dynamic_slice.15
  147.5 12.4 %collective-permute-start.7 = (bf16[2,128,1024]{2,1,0:T(8,128)(2,1)}, bf16[2,128,1024]{2,1,0:T(8,128)(2,1)}, u32[]{:S(2)}, u32[]{:S(2)}) collective-permute-start(bf16[2,128,1024]{2,1,0:T(8,128)(2,1)} %collective-permute-done.6), channel_id=1, source_target_pairs={{0,1},{1,2},{2,3},{3,4},{4,5},{5,6},{6,7},{7,8},{8,9},{9,10},{10,1... | collective-permute-start | bytes 1572872 | tf_op jit(solution)/shard_map/ppermute | solution.py:15
  159.9 0.6 broadcast_compare_fusion
  160.5 0.6 fusion.54
  161.4 1.1 constant_dynamic-update-slice_fusion.8
  162.5 1.1 constant_dynamic-update-slice_fusion.7
  163.6 1.1 constant_dynamic-update-slice_fusion.6
  164.7 1.1 constant_dynamic-update-slice_fusion.5
  166.0 2.0 fusion.57
  167.9 4.4 %copy.15 = bf16[1,1152,1024]{1,2,0:T(8,128)(2,1)} copy(bf16[1,1152,1024]{2,1,0:T(8,128)(2,1)} %get-tuple-element.93) | data formatting | bytes 4718592 | tf_op jit(solution)/shard_map/slice | solution.py:87
  172.3 2.6 copy.17
  174.9 15.3 %while.11 = (s32[]{:T(128)}, bf16[4,128,4,64]{1,3,2,0:T(8,128)(2,1)S(1)}, bf16[4,1152,4,64]{1,3,2,0:T(8,128)(2,1)}, bf16[4,128,4,64]{1,3,2,0:T(8,128)(2,1)S(1)},...) while((s32[]{:T(128)}, ...), condition=%wide.region_4.5_spmd.clone, body=%wide.region_2.4_spmd.clone.sunk | while | flops 154420864 | bytes 8694133 | solution.py:102
  175.2 1.7 fusion.76
  177.0 1.7 fusion.77
  179.0 1.7 fusion.76
  180.8 1.7 fusion.77
  182.9 1.7 fusion.76
  184.6 1.7 fusion.77
  186.7 1.8 fusion.76
  188.5 1.7 fusion.77
  190.3 2.1 convert_reduce_fusion
  192.7 7.6 %all-gather.8.cloned.1.call-done = bf16[1024,2048]{1,0:T(8,128)(2,1)} async-done(((bf16[64,2048]{1,0:T(8,128)(2,1)}), bf16[1024,2048]{1,0:T(8,128)(2,1)}) %all-gather.8.cloned.1.call-update) | async-done | bytes 4194320 | tf_op jit(solution)/shard_map/all_gather | solution.py:109
  200.3 3.0 %fusion.45 = f32[128,2048]{1,0:T(8,128)S(1)} fusion(bf16[1024,2048]{1,0:T(8,128)(2,1)} %all-gather.8.cloned.1.call-done, bf16[128,1024]{1,0:T(8,128)(2,1)S(1)} %get-tuple-element.111, f32[1024]{0:T(1024)S(1)} %copy-done.7, f32[128]{0:T(128)S(1)} %add_rsqrt_fusion.1, f32[128]{0:T(128)S(1)} %broadcast_multiply_fusion), kind=kOutput, calls=%fused_computation.64 | convolution fusion | flops 537526272 | bytes 5510144 | tf_op jit(solution)/shard_map/dot_general | solution.py:43
  203.4 2.2 collective-permute-start.8
  205.6 1.3 collective-permute-start.9
  208.2 5.3 %collective-permute-done.9 = bf16[4,1024]{1,0:T(4,128)(2,1)S(1)} collective-permute-done((bf16[4,1024]{1,0:T(4,128)(2,1)S(1)}, bf16[4,1024]{1,0:T(4,128)(2,1)S(1)}, u32[]{:S(2)}, u32[]{:S(2)}) %collective-permute-start.9) | collective-permute-done | bytes 8224 | tf_op jit(solution)/shard_map/ppermute | solution.py:28
  213.6 0.7 select_reduce_fusion
  214.3 66.7 %all-reduce = (f32[1024]{0:T(1024)S(1)}, f32[1024]{0:T(1024)S(1)}) all-reduce(f32[1024]{0:T(1024)S(1)} %get-tuple-element.66, f32[1024]{0:T(1024)S(1)} %get-tuple-element.65), channel_id=1, replica_groups=mesh['call'=2,'tm'=16] {'call','tm'}, use_global_device_ids=true, to_apply=%region_11.12 | all-reduce | flops 2048 | bytes 16384 | tf_op jit(solution)/shard_map/psum | solution.py:120
  281.0 0.9 fusion.53
  (52 shorter events, 3.3 us)
Async XLA Ops:
  7.2 67.7 %all-gather.4.cloned.1.call-start = ((), (), s32[]{:S(2)}) async-start(), calls=%async_computation | async-start | bytes 6684672 | tf_op jit(solution)/shard_map/all_gather | solution.py:58
  7.9 182.3 %all-gather.6.cloned.1.call-start = ((), (), s32[]{:S(2)}) async-start(), calls=%async_computation.1 | async-start | bytes 2228224 | tf_op jit(solution)/shard_map/all_gather | solution.py:104
  8.6 191.6 %all-gather.8.cloned.1.call-start = ((), (), s32[]{:S(2)}) async-start(), calls=%async_computation.2 | async-start | bytes 4456448 | tf_op jit(solution)/shard_map/all_gather | solution.py:109
  10.9 135.5 %copy-start.8 = (s32[2]{0:T(128)S(1)}, s32[2]{0:T(128)}, u32[]{:S(2)}) copy-start(s32[2]{0:T(128)} %param.13) | copy-start | bytes 28
  79.0 3.7 %collective-permute-start = (bf16[2,128,1024]{2,1,0:T(8,128)(2,1)S(1)}, bf16[2,128,1024]{2,1,0:T(8,128)(2,1)S(1)}, u32[]{:S(2)}, u32[]{:S(2)}) collective-permute-start(bf16[2,128,1024]{2,1,0:T(8,128)(2,1)S(1)} %pad_maximum_fusion), channel_id=1, source_target_pairs={{0,1},{1,2},{2,3},{3,4},{4,5},{5,6},{6,7},{7,8},{8,9},{9,10},{10,1... | collective-permute-start | bytes 1572872 | tf_op jit(solution)/shard_map/ppermute | solution.py:15
  82.6 9.8 %collective-permute-start.1 = (bf16[2,128,1024]{2,1,0:T(8,128)(2,1)S(1)}, bf16[2,128,1024]{2,1,0:T(8,128)(2,1)S(1)}, u32[]{:S(2)}, u32[]{:S(2)}) collective-permute-start(bf16[2,128,1024]{2,1,0:T(8,128)(2,1)S(1)} %collective-permute-done), channel_id=1, source_target_pairs={{0,1},{1,2},{2,3},{3,4},{4,5},{5,6},{6,7},{7,8},{8,9},{9,10},{10,1... | collective-permute-start | bytes 1572872 | tf_op jit(solution)/shard_map/ppermute | solution.py:15
  92.5 10.5 %collective-permute-start.2 = (bf16[2,128,1024]{2,1,0:T(8,128)(2,1)S(1)}, bf16[2,128,1024]{2,1,0:T(8,128)(2,1)S(1)}, u32[]{:S(2)}, u32[]{:S(2)}) collective-permute-start(bf16[2,128,1024]{2,1,0:T(8,128)(2,1)S(1)} %collective-permute-done.1), channel_id=1, source_target_pairs={{0,1},{1,2},{2,3},{3,4},{4,5},{5,6},{6,7},{7,8},{8,9},{9,10},{10,1... | collective-permute-start | bytes 1572872 | tf_op jit(solution)/shard_map/ppermute | solution.py:15
  103.0 12.7 %collective-permute-start.3 = (bf16[2,128,1024]{2,1,0:T(8,128)(2,1)S(1)}, bf16[2,128,1024]{2,1,0:T(8,128)(2,1)S(1)}, u32[]{:S(2)}, u32[]{:S(2)}) collective-permute-start(bf16[2,128,1024]{2,1,0:T(8,128)(2,1)S(1)} %collective-permute-done.2), channel_id=1, source_target_pairs={{0,1},{1,2},{2,3},{3,4},{4,5},{5,6},{6,7},{7,8},{8,9},{9,10},{10,1... | collective-permute-start | bytes 1572872 | tf_op jit(solution)/shard_map/ppermute | solution.py:15
  115.6 10.5 %collective-permute-start.4 = (bf16[2,128,1024]{2,1,0:T(8,128)(2,1)S(1)}, bf16[2,128,1024]{2,1,0:T(8,128)(2,1)S(1)}, u32[]{:S(2)}, u32[]{:S(2)}) collective-permute-start(bf16[2,128,1024]{2,1,0:T(8,128)(2,1)S(1)} %collective-permute-done.3), channel_id=1, source_target_pairs={{0,1},{1,2},{2,3},{3,4},{4,5},{5,6},{6,7},{7,8},{8,9},{9,10},{10,1... | collective-permute-start | bytes 1572872 | tf_op jit(solution)/shard_map/ppermute | solution.py:15
  126.1 35.1 %copy-start.2 = (bf16[2,128,1024]{2,1,0:T(8,128)(2,1)}, bf16[2,128,1024]{2,1,0:T(8,128)(2,1)S(1)}, u32[]{:S(2)}) copy-start(bf16[2,128,1024]{2,1,0:T(8,128)(2,1)S(1)} %collective-permute-done.4) | copy-start | bytes 1572868
  126.1 10.6 %collective-permute-start.5 = (bf16[2,128,1024]{2,1,0:T(8,128)(2,1)S(1)}, bf16[2,128,1024]{2,1,0:T(8,128)(2,1)}, u32[]{:S(2)}, u32[]{:S(2)}) collective-permute-start(bf16[2,128,1024]{2,1,0:T(8,128)(2,1)S(1)} %collective-permute-done.4), channel_id=1, source_target_pairs={{0,1},{1,2},{2,3},{3,4},{4,5},{5,6},{6,7},{7,8},{8,9},{9,10},{10,1... | collective-permute-start | bytes 1572872 | tf_op jit(solution)/shard_map/ppermute | solution.py:15
  136.8 10.7 %collective-permute-start.6 = (bf16[2,128,1024]{2,1,0:T(8,128)(2,1)}, bf16[2,128,1024]{2,1,0:T(8,128)(2,1)}, u32[]{:S(2)}, u32[]{:S(2)}) collective-permute-start(bf16[2,128,1024]{2,1,0:T(8,128)(2,1)} %collective-permute-done.5), channel_id=1, source_target_pairs={{0,1},{1,2},{2,3},{3,4},{4,5},{5,6},{6,7},{7,8},{8,9},{9,10},{10,1... | collective-permute-start | bytes 1572872 | tf_op jit(solution)/shard_map/ppermute | solution.py:15
  147.5 13.9 %collective-permute-start.7 = (bf16[2,128,1024]{2,1,0:T(8,128)(2,1)}, bf16[2,128,1024]{2,1,0:T(8,128)(2,1)}, u32[]{:S(2)}, u32[]{:S(2)}) collective-permute-start(bf16[2,128,1024]{2,1,0:T(8,128)(2,1)} %collective-permute-done.6), channel_id=1, source_target_pairs={{0,1},{1,2},{2,3},{3,4},{4,5},{5,6},{6,7},{7,8},{8,9},{9,10},{10,1... | collective-permute-start | bytes 1572872 | tf_op jit(solution)/shard_map/ppermute | solution.py:15
  167.9 7.0 %copy-start.3 = (bf16[4,128,4,64]{1,3,2,0:T(8,128)(2,1)S(1)}, bf16[4,128,4,64]{1,3,2,0:T(8,128)(2,1)}, u32[]{:S(2)}) copy-start(bf16[4,128,4,64]{1,3,2,0:T(8,128)(2,1)} %custom-call.1) | copy-start | bytes 786436
  174.9 15.3 %copy-start = (bf16[1,128,1024]{2,1,0:T(8,128)(2,1)S(1)}, bf16[1,128,1024]{2,1,0:T(8,128)(2,1)}, u32[]{:S(2)}) copy-start(bf16[1,128,1024]{2,1,0:T(8,128)(2,1)} %param.12) | copy-start | bytes 786436
  174.9 25.3 %copy-start.7 = (f32[1024]{0:T(1024)S(1)}, f32[1024]{0:T(1024)}, u32[]{:S(2)}) copy-start(f32[1024]{0:T(1024)} %param.17) | copy-start | bytes 12292
  192.4 89.5 %copy-start.1 = (bf16[128,1024]{1,0:T(8,128)(2,1)}, bf16[128,1024]{1,0:T(8,128)(2,1)S(1)}, u32[]{:S(2)}) copy-start(bf16[128,1024]{1,0:T(8,128)(2,1)S(1)} %get-tuple-element.111) | copy-start | bytes 786436
  192.4 14.5 %copy-start.4 = (f32[9,1024]{1,0:T(8,128)S(1)}, f32[9,1024]{1,0:T(8,128)}, u32[]{:S(2)}) copy-start(f32[9,1024]{1,0:T(8,128)} %param.19) | copy-start | bytes 110596
  192.4 88.5 %copy-start.5 = (f32[1024]{0:T(1024)S(1)}, f32[1024]{0:T(1024)}, u32[]{:S(2)}) copy-start(f32[1024]{0:T(1024)} %param.21) | copy-start | bytes 12292
  192.4 88.5 %copy-start.6 = (f32[1024]{0:T(1024)S(1)}, f32[1024]{0:T(1024)}, u32[]{:S(2)}) copy-start(f32[1024]{0:T(1024)} %param.20) | copy-start | bytes 12292
  203.4 4.8 %collective-permute-start.8 = (bf16[4,1024]{1,0:T(4,128)(2,1)S(1)}, bf16[4,1024]{1,0:T(4,128)(2,1)S(1)}, u32[]{:S(2)}, u32[]{:S(2)}) collective-permute-start(bf16[4,1024]{1,0:T(4,128)(2,1)S(1)} %get-tuple-element.97), channel_id=1, source_target_pairs={{0,1},{1,2},{2,3},{3,4},{4,5},{5,6},{6,7},{7,8},{8,9},{9,10},{10,1... | collective-permute-start | bytes 24584 | tf_op jit(solution)/shard_map/ppermute | solution.py:26
  205.6 8.0 %collective-permute-start.9 = (bf16[4,1024]{1,0:T(4,128)(2,1)S(1)}, bf16[4,1024]{1,0:T(4,128)(2,1)S(1)}, u32[]{:S(2)}, u32[]{:S(2)}) collective-permute-start(bf16[4,1024]{1,0:T(4,128)(2,1)S(1)} %get-tuple-element.98), channel_id=1, source_target_pairs={{1,0},{2,1},{3,2},{4,3},{5,4},{6,5},{7,6},{8,7},{9,8},{10,9},{11,1... | collective-permute-start | bytes 24584 | tf_op jit(solution)/shard_map/ppermute | solution.py:28
Sparse Core Ops, SparseCore 0:
  10.3 64.5 all-gather.3
  77.0 40.8 all-gather.5
  136.1 64.1 all-gather.7
where the time goes:
time: 290 us; the launch traced here: 288 us
  waiting for transfers between devices  86.9 us (30%)
  starting transfers between devices  75.1 us (26%)
  blocking collectives  66.7 us (23%)
  matrix products  23.1 us (8%)
  between operations  14.7 us (5%)
  local copies, waits for them, and re-layouts  14.4 us (5%)
  other arithmetic  7.46 us (3%)
    ppermute x8, starting transfers between devices, passed_along(): lax.ppermute(value, axis, [(source, source + steps) for source in range(f...  71.6 us
    psum x1, blocking collectives, on_device(): lax.psum((jnp.sum(masked, axis=0), jnp.sum(masked * depthwise, axis=0)),...  66.7 us
    all_gather x1, waiting for transfers between devices, on_device(): lax.all_gather(w_qkv, 'tm', axis=0, tiled=True)  63.9 us
    dot_general x3, matrix products, contract_with(): return jnp.dot(left, rows_piece, preferred_element_type=jnp.float32)  9.08 us
    ppermute x8, waiting for transfers between devices, passed_along(): lax.ppermute(value, axis, [(source, source + steps) for source in range(f...  8.63 us
    all_gather x1, waiting for transfers between devices, on_device(): lax.all_gather(w_pw1, 'tm', axis=0, tiled=True)  7.56 us
    dot_general x4, matrix products, attend_group(): jnp.einsum('hqk,khd->qhd', probs, value_part, preferred_element_type=jnp....  6.99 us
    dot_general x4, matrix products, attend_group(): jnp.einsum('qhd,khd->hqk', query_part, key_part, preferred_element_type=j...  6.98 us
  transfers between devices with their start and end apart: 13, of which 10 were waited for; matrix products, arithmetic and copies ran while one was open for 14% of the time, Pallas kernels for 0%

commit v1 on v0

--- a/solution.py
+++ b/solution.py
@@ -1,6 +1,10 @@
+import functools
+
 import jax
 import jax.numpy as jnp
 from jax import lax
+from jax.experimental import pallas as pl
+from jax.experimental.pallas import tpu as pltpu
 from jax.sharding import PartitionSpec as P
 
 HEAD_DIM = 64
@@ -131,9 +135,350 @@
     return (attended[None], conv_act[None])
 
 
+MESH = pl.DeviceIdType.MESH
+
+
+def remote(source, target, send_sem, recv_sem, where):
+    return pltpu.make_async_remote_copy(
+        src_ref=source,
+        dst_ref=target,
+        send_sem=send_sem,
+        recv_sem=recv_sem,
+        device_id=where,
+        device_id_type=MESH,
+    )
+
+
+def greet(places):
+    barrier = pltpu.get_barrier_semaphore()
+    for where in places:
+        pl.semaphore_signal(barrier, inc=1, device_id=where, device_id_type=MESH)
+    pl.semaphore_wait(barrier, len(places))
+
+
+def gather_kernel(count, x_ref, w_ref, xall, wcol, send_x, recv_x, send_w, recv_w, own_sem):
+    me = lax.axis_index("tm")
+    y_peer = me + 2 - 4 * ((me // 2) % 2)
+    c_peer = me + 1 - 2 * (me % 2)
+    both = y_peer + 1 - 2 * (me % 2)
+    greet([{"tm": (me + step) % count} for step in range(1, count)])
+    own_x = pltpu.make_async_copy(x_ref, xall.at[me], own_sem.at[0])
+    own_w = pltpu.make_async_copy(w_ref.at[me], wcol.at[me], own_sem.at[1])
+    own_x.start()
+    own_w.start()
+    sends = []
+
+    def push(source, owner, place):
+        copy = remote(
+            source, xall.at[owner], send_x.at[len(sends)], recv_x.at[owner], {"tm": place}
+        )
+        copy.start()
+        sends.append(copy)
+
+    def arrived(owner):
+        remote(
+            xall.at[owner], xall.at[owner], send_x.at[0], recv_x.at[owner], {"tm": c_peer}
+        ).wait_recv()
+
+    hops = range(4, count, 4)
+    push(x_ref, me, y_peer)
+    for hop in hops:
+        push(x_ref, me, (me + hop) % count)
+    push(x_ref, me, c_peer)
+    w_sends = []
+    for step in range(1, count):
+        place = (me + step) % count
+        copy = remote(
+            w_ref.at[place], wcol.at[me], send_w.at[step], recv_w.at[me], {"tm": place}
+        )
+        copy.start()
+        w_sends.append(copy)
+    arrived(y_peer)
+    push(xall.at[y_peer], y_peer, c_peer)
+    for hop in hops:
+        owner = (me + hop) % count
+        arrived(owner)
+        push(xall.at[owner], owner, y_peer)
+        push(xall.at[owner], owner, c_peer)
+    for hop in hops:
+        owner = (y_peer + hop) % count
+        arrived(owner)
+        push(xall.at[owner], owner, c_peer)
+    arrived(c_peer)
+    arrived(both)
+    for hop in hops:
+        arrived((c_peer + hop) % count)
+        arrived((both + hop) % count)
+    for step in range(1, count):
+        owner = (me + step) % count
+        remote(
+            w_ref.at[owner], wcol.at[owner], send_w.at[0], recv_w.at[owner], {"tm": c_peer}
+        ).wait_recv()
+    for copy in sends + w_sends:
+        copy.wait_send()
+    own_x.wait()
+    own_w.wait()
+
+
+def gather_call(normed, w_heads):
+    count = w_heads.shape[0]
+    anywhere = pl.BlockSpec(memory_space=pl.ANY)
+    return pl.pallas_call(
+        functools.partial(gather_kernel, count),
+        out_shape=(
+            jax.ShapeDtypeStruct((count,) + normed.shape, normed.dtype),
+            jax.ShapeDtypeStruct(w_heads.shape, w_heads.dtype),
+        ),
+        in_specs=[anywhere] * 2,
+        out_specs=(anywhere, anywhere),
+        scratch_shapes=[
+            pltpu.SemaphoreType.DMA((count,)),
+            pltpu.SemaphoreType.DMA((count,)),
+            pltpu.SemaphoreType.DMA((count,)),
+            pltpu.SemaphoreType.DMA((count,)),
+            pltpu.SemaphoreType.DMA((2,)),
+        ],
+        compiler_params=pltpu.CompilerParams(collective_id=0, has_side_effects=True),
+        name="gather_frames",
+    )(normed, w_heads)
+
+
+def attend_kernel(scale, length_ref, q_ref, k_ref, v_ref, out_ref):
+    block = pl.program_id(0)
+    width = LEFT + SPAN
+    first = pl.multiple_of(block * SPAN, SPAN)
+    keys = k_ref[pl.ds(first, width), :]
+    scores = lax.dot_general(
+        q_ref[...], keys, (((1,), (1,)), ((), ())), preferred_element_type=jnp.float32
+    )
+    key_pos = block * SPAN - LEFT + lax.broadcasted_iota(jnp.int32, (SPAN, width), 1)
+    query_pos = block * SPAN + lax.broadcasted_iota(jnp.int32, (SPAN, width), 0)
+    allowed = (key_pos >= 0) & ((key_pos < length_ref[0]) | (key_pos == query_pos))
+    raised = jnp.where(allowed, jnp.exp(scores * scale), 0.0)
+    probs = (raised / jnp.sum(raised, axis=-1, keepdims=True)).astype(jnp.bfloat16)
+    mixed = jnp.dot(probs, v_ref[pl.ds(first, width), :], preferred_element_type=jnp.float32)
+    out_ref[0] = mixed.astype(jnp.bfloat16)
+
+
+def attend_call(length, queries, keys, values):
+    frames, width = queries.shape
+    count = frames // SPAN
+    whole = pl.BlockSpec((frames + LEFT, width), lambda i: (0, 0))
+    return pl.pallas_call(
+        functools.partial(attend_kernel, HEAD_DIM**-0.5),
+        grid=(count,),
+        out_shape=jax.ShapeDtypeStruct((count, SPAN, width), jnp.bfloat16),
+        in_specs=[
+            pl.BlockSpec(memory_space=pltpu.SMEM),
+            pl.BlockSpec((SPAN, width), lambda i: (i, 0)),
+            whole,
+            whole,
+        ],
+        out_specs=pl.BlockSpec((1, SPAN, width), lambda i: (i, 0, 0)),
+        compiler_params=pltpu.CompilerParams(vmem_limit_bytes=32 * 1024 * 1024),
+        name="attend_head",
+    )(length, queries, keys, values)
+
+
+def exchange_kernel(count, x_ref, out_ref, send, recv, own_sem):
+    me = lax.axis_index("tm")
+    greet([{"tm": (me + step) % count} for step in range(1, count)])
+    own = pltpu.make_async_copy(x_ref.at[me], out_ref.at[me], own_sem.at[0])
+    own.start()
+    sends = []
+    for step in range(1, count):
+        place = (me + step) % count
+        copy = remote(x_ref.at[place], out_ref.at[me], send.at[step], recv.at[me], {"tm": place})
+        copy.start()
+        sends.append(copy)
+    for step in range(1, count):
+        owner = (me + step) % count
+        remote(
+            x_ref.at[owner], out_ref.at[owner], send.at[0], recv.at[owner], {"tm": owner}
+        ).wait_recv()
+    for copy in sends:
+        copy.wait_send()
+    own.wait()
+
+
+def exchange_call(blocks):
+    count = blocks.shape[0]
+    anywhere = pl.BlockSpec(memory_space=pl.ANY)
+    return pl.pallas_call(
+        functools.partial(exchange_kernel, count),
+        out_shape=jax.ShapeDtypeStruct(blocks.shape, blocks.dtype),
+        in_specs=[anywhere],
+        out_specs=anywhere,
+        scratch_shapes=[
+            pltpu.SemaphoreType.DMA((count,)),
+            pltpu.SemaphoreType.DMA((count,)),
+            pltpu.SemaphoreType.DMA((1,)),
+        ],
+        compiler_params=pltpu.CompilerParams(collective_id=1, has_side_effects=True),
+        name="exchange_context",
+    )(blocks)
+
+
+EDGE = 16
+STRIP = 128
+
+
+def conv_kernel(
+    count, g_ref, valid_ref, total_ref, taps_ref, gain_ref, bias_ref, out_ref,
+    low, high, padded, depth, mine, plane, near, far,
+    halo_send, halo_recv, near_send, near_recv, far_send, far_recv,
+):
+    me = lax.axis_index("tm")
+    call = lax.axis_index("call")
+    rows, width = depth.shape
+    right, left = (me + 1) % count, (me + count - 1) % count
+    peers = []
+    for flips in range(1, 8):
+        spot, side = me, call
+        if flips & 1:
+            spot = spot + 1 - 2 * (me % 2)
+        if flips & 2:
+            spot = spot + 2 - 4 * ((me // 2) % 2)
+        if flips & 4:
+            side = 1 - call
+        peers.append({"call": side, "tm": spot})
+    hops = [{"tm": (me + hop) % count} for hop in range(4, count, 4)]
+    greet([{"tm": right}, {"tm": left}] + peers + hops)
+    to_right = remote(
+        g_ref.at[pl.ds(rows - EDGE, EDGE)], low, halo_send.at[0], halo_recv.at[0], {"tm": right}
+    )
+    to_left = remote(
+        g_ref.at[pl.ds(0, EDGE)], high, halo_send.at[1], halo_recv.at[1], {"tm": left}
+    )
+    to_right.start()
+    to_left.start()
+    padded[EDGE : EDGE + rows, :] = g_ref[...].astype(jnp.float32)
+    to_right.wait_recv()
+    to_left.wait_recv()
+    has_low = jnp.where(me > 0, 1.0, 0.0).astype(jnp.float32)
+    has_high = jnp.where(me < count - 1, 1.0, 0.0).astype(jnp.float32)
+    padded[0:EDGE, :] = low[...].astype(jnp.float32) * has_low
+    padded[EDGE + rows : 2 * EDGE + rows, :] = high[...].astype(jnp.float32) * has_high
+    valid = valid_ref[...]
+    for at in range(0, width, STRIP):
+        strip = slice(at, at + STRIP)
+        total = jnp.zeros((rows, STRIP), jnp.float32)
+        for tap in range(KERNEL):
+            start = EDGE - KERNEL // 2 + tap
+            total = total + padded[start : start + rows, strip] * taps_ref[tap : tap + 1, strip]
+        depth[:, strip] = total
+        masked = total * valid
+        mine[0:1, strip] = jnp.sum(masked, axis=0, keepdims=True)
+        mine[1:2, strip] = jnp.sum(masked * total, axis=0, keepdims=True)
+    near_copies = []
+    for slot, where in enumerate(peers):
+        copy = remote(mine, near.at[slot], near_send.at[slot], near_recv.at[slot], where)
+        copy.start()
+        near_copies.append(copy)
+    for copy in near_copies:
+        copy.wait_recv()
+    both = mine[...]
+    for slot in range(len(peers)):
+        both = both + near[slot]
+    plane[...] = both
+    far_copies = []
+    for slot, where in enumerate(hops):
+        copy = remote(plane, far.at[slot], far_send.at[slot], far_recv.at[slot], where)
+        copy.start()
+        far_copies.append(copy)
+    for copy in far_copies:
+        copy.wait_recv()
+    for slot in range(len(hops)):
+        both = both + far[slot]
+    both = both / total_ref[...]
+    average = both[0:1]
+    spread = lax.rsqrt(both[1:2] - average * average + 1e-05)
+    for at in range(0, width, STRIP):
+        strip = slice(at, at + STRIP)
+        act = (depth[:, strip] - average[:, strip]) * spread[:, strip]
+        act = act * gain_ref[:, strip] + bias_ref[:, strip]
+        act = act * jax.nn.sigmoid(act)
+        out_ref[:, strip] = jnp.where(valid > 0.0, act, 0.0).astype(out_ref.dtype)
+    for copy in [to_right, to_left] + near_copies + far_copies:
+        copy.wait_send()
+
+
+def conv_call(count, gated, valid, total, taps, gain, bias):
+    rows, width = gated.shape
+    vmem = pl.BlockSpec(memory_space=pltpu.VMEM)
+    sems = pltpu.SemaphoreType.DMA
+    far_count = count // 4 - 1
+    return pl.pallas_call(
+        functools.partial(conv_kernel, count),
+        out_shape=jax.ShapeDtypeStruct(gated.shape, jnp.bfloat16),
+        in_specs=[vmem] * 6,
+        out_specs=vmem,
+        scratch_shapes=[
+            pltpu.VMEM((EDGE, width), jnp.bfloat16),
+            pltpu.VMEM((EDGE, width), jnp.bfloat16),
+            pltpu.VMEM((rows + 2 * EDGE, width), jnp.float32),
+            pltpu.VMEM((rows, width), jnp.float32),
+            pltpu.VMEM((2, width), jnp.float32),
+            pltpu.VMEM((2, width), jnp.float32),
+            pltpu.VMEM((7, 2, width), jnp.float32),
+            pltpu.VMEM((far_count, 2, width), jnp.float32),
+            sems((2,)), sems((2,)), sems((7,)), sems((7,)), sems((far_count,)), sems((far_count,)),
+        ],
+        compiler_params=pltpu.CompilerParams(
+            collective_id=2, has_side_effects=True, vmem_limit_bytes=32 * 1024 * 1024
+        ),
+        name="conv_norm",
+    )(gated, valid, total, taps, gain, bias)
+
+
+def one_head_each(
+    frames, lengths, ln_attn_gain, w_qkv, w_out, ln_conv_gain, w_pw1, dw_kernel, bn_gain, bn_bias
+):
+    stream = frames[0]
+    frame_count, model_width = stream.shape
+    count = lax.axis_size("tm")
+    length = lax.dynamic_index_in_dim(lengths, lax.axis_index("call"), 0, keepdims=False)
+    query_pos = lax.axis_index("tm") * frame_count + jnp.arange(frame_count, dtype=jnp.int32)
+    frame_valid = (query_pos < length)[:, None]
+    normed = layer_norm(stream, ln_attn_gain).astype(jnp.bfloat16)
+    w_heads = w_qkv.reshape(-1, 3, count, HEAD_DIM).transpose(2, 0, 1, 3)
+    w_heads = w_heads.reshape(count, -1, 3 * HEAD_DIM)
+    all_frames, w_columns = gather_call(normed, w_heads)
+    packed = contract_with(
+        all_frames.reshape(-1, model_width), w_columns.reshape(model_width, -1)
+    ).astype(jnp.bfloat16)
+    queries = packed[:, :HEAD_DIM]
+    keys = jnp.pad(packed[:, HEAD_DIM : 2 * HEAD_DIM], ((LEFT, 0), (0, 0)))
+    values = jnp.pad(packed[:, 2 * HEAD_DIM :], ((LEFT, 0), (0, 0)))
+    blocks = attend_call(length[None], queries, keys, values)
+    context = exchange_call(blocks).transpose(1, 0, 2).reshape(frame_count, model_width)
+    projected = contract_with(context, lax.all_gather(w_out, "tm", axis=0, tiled=True))
+    attended = jnp.where(frame_valid, stream.astype(jnp.float32) + projected, 0.0).astype(
+        jnp.bfloat16
+    )
+    conv_in = layer_norm(attended, ln_conv_gain).astype(jnp.bfloat16)
+    expanded = contract_with(conv_in, lax.all_gather(w_pw1, "tm", axis=0, tiled=True))
+    gated = expanded[:, :model_width] * jax.nn.sigmoid(expanded[:, model_width:])
+    gated = jnp.where(frame_valid, gated, 0.0).astype(jnp.bfloat16)
+    conv_act = conv_call(
+        count,
+        gated,
+        frame_valid.astype(jnp.float32),
+        jnp.sum(lengths).astype(jnp.float32).reshape(1, 1),
+        dw_kernel,
+        bn_gain[None],
+        bn_bias[None],
+    )
+    return (attended[None], conv_act[None])
+
+
+def fits_one_head(mesh):
+    return mesh.shape["tm"] == 16 and mesh.shape["call"] == 2
+
+
 def solution(mesh):
     return jax.shard_map(
-        on_device,
+        one_head_each if fits_one_head(mesh) else on_device,
         mesh=mesh,
         in_specs=(
             P("call", "tm", None),

time: 290 us -> 156 us (0.54)
  Pallas kernels: 0 us -> 110 us
  waiting for transfers between devices: 86.9 us -> 10.3 us
  starting transfers between devices: 75.1 us -> 0.08 us
  blocking collectives: 66.7 us -> 0 us
  matrix products: 23.1 us -> 8.82 us
  local copies, waits for them, and re-layouts: 14.4 us -> 8.09 us
  other arithmetic: 7.46 us -> 4.34 us
    pallas_call x0 -> x4, Pallas kernels: none -> 110 us  [the longest x1 54.2 us: gather_call(): pl.pallas_call(functools.partial(gather_kernel, count), out_shape=(jax.Sh...]
    ppermute x10 -> x0, starting transfers between devices: 75 us -> none  [the longest x8 71.6 us: passed_along(): lax.ppermute(value, axis, [(source, source + steps) for source in range(f...]
    psum x1 -> x0, blocking collectives: 66.7 us -> none  [on_device(): lax.psum((jnp.sum(masked, axis=0), jnp.sum(masked * depthwise, axis=0)),...]
    all_gather x3 -> x2, waiting for transfers between devices: 71.5 us -> 8.93 us  [the longest x1 8.91 us: one_head_each(): lax.all_gather(w_pw1, 'tm', axis=0, tiled=True)]
    dot_general x8 -> x0, matrix products: 14 us -> none  [the longest x4 6.99 us: attend_group(): jnp.einsum('hqk,khd->qhd', probs, value_part, preferred_element_type=jnp....]
    ppermute x10 -> x0, waiting for transfers between devices: 14 us -> none  [the longest x8 8.63 us: passed_along(): lax.ppermute(value, axis, [(source, source + steps) for source in range(f...]
    slice x7 -> x1, local copies, waits for them, and re-layouts: 9.22 us -> 0.33 us  [one_head_each(): values = jnp.pad(packed[:, 2 * HEAD_DIM:], ((LEFT, 0), (0, 0)))]
    reshape x0 -> x3, local copies, waits for them, and re-layouts: none -> 3.48 us  [the longest x2 2.32 us: one_head_each(): w_heads = w_qkv.reshape(-1, 3, count, HEAD_DIM).transpose(2, 0, 1, 3)]
  transfers between devices with their start and end apart: 13 -> 2, of which waited for: 10 -> 1; matrix products, arithmetic and copies ran while one was open for 14% -> 11% of each run, Pallas kernels for 0% -> 61%
where the time goes in v1:
time: 156 us
  Pallas kernels  110 us (71%)
  between operations  14.9 us (10%)
  waiting for transfers between devices  10.3 us (7%)
  matrix products  8.82 us (6%)
  local copies, waits for them, and re-layouts  8.09 us (5%)
  other arithmetic  4.34 us (3%)
    pallas_call x1, Pallas kernels, gather_call(): pl.pallas_call(functools.partial(gather_kernel, count), out_shape=(jax.Sh...  54.2 us
    pallas_call x1, Pallas kernels, exchange_call(): pl.pallas_call(functools.partial(exchange_kernel, count), out_shape=jax.S...  31.5 us
    pallas_call x1, Pallas kernels, conv_call(): pl.pallas_call(functools.partial(conv_kernel, count), out_shape=jax.Shape...  13.6 us
    pallas_call x1, Pallas kernels, attend_call(): pl.pallas_call(functools.partial(attend_kernel, HEAD_DIM ** (-0.5)), grid...  10.2 us
    all_gather x1, waiting for transfers between devices, one_head_each(): lax.all_gather(w_pw1, 'tm', axis=0, tiled=True)  8.91 us
    dot_general x3, matrix products, contract_with(): return jnp.dot(left, rows_piece, preferred_element_type=jnp.float32)  8.82 us
  transfers between devices with their start and end apart: 2, of which 1 were waited for; matrix products, arithmetic and copies ran while one was open for 11% of the time, Pallas kernels for 61%

profile of v1, /device:TPU:0, one launch (start us, length us, event | category | flops | bytes accessed | tf_op | source)
XLA Modules:
  0.0 156.1 jit_solution(5796974427688407569)
XLA Ops:
  7.2 0.0 copy-start.4
  7.2 0.0 copy-start.6
  7.2 0.0 all-gather.3.cloned.1.call-start
  7.2 0.7 all-gather.3.cloned.1.call-update
  7.9 0.0 all-gather.5.cloned.1.call-start
  8.0 0.7 all-gather.5.cloned.1.call-update
  8.7 1.4 reduce_sum.49
  10.0 1.2 dynamic_slice.4.length_ref
  11.3 1.5 reshape.65
  12.8 0.8 copy.18
  13.6 1.2 copy.19.w_ref
  14.8 0.0 copy-done.4
  14.8 0.1 convert_reduce_fusion.1
  14.9 0.2 fusion.10
  15.1 0.0 copy-done.6
  15.1 0.9 fusion.12.x_ref
  16.1 54.2 %gather_frames.1 = (bf16[16,128,1024]{2,1,0:T(8,128)(2,1)}, bf16[16,64,192]{2,1,0:T(8,128)(2,1)}) custom-call(bf16[128,1024]{1,0:T(8,128)(2,1)} %fusion.12.x_ref, bf16[16,64,192]{2,1,0:T(8,128)(2,1)} %copy.19.w_ref), custom_call_target="tpu_custom_call" | custom-call | tf_op jit(solution)/shard_map/gather_frames/pallas_call | solution.py:226
  70.3 3.7 %convolution_convert_fusion = bf16[2048,192]{1,0:T(8,128)(2,1)S(1)} fusion(bf16[2048,1024]{1,0:T(8,128)(2,1)} %bitcast.41, bf16[1024,192]{1,0:T(8,128)(2,1)} %bitcast.42), kind=kOutput, calls=%fused_computation | convolution fusion | flops 805699584 | bytes 5373952 | tf_op jit(solution)/shard_map/dot_general | solution.py:47
  73.9 0.3 fusion.25
  74.3 0.1 pad.7.k_ref
  74.4 0.0 copy-start.7
  74.4 0.1 pad.8.v_ref
  74.6 10.2 %attend_head.1.x_ref = bf16[16,128,64]{2,1,0:T(8,128)(2,1)S(1)} custom-call(s32[1]{0:T(128)} %dynamic_slice.4.length_ref, bf16[2048,64]{1,0:T(8,128)(2,1)S(1)} %get-tuple-element.8.q_ref, bf16[3072,64]{1,0:T(8,128)(2,1)S(1)} %pad.7.k_ref, bf16[3072,64]{1,0:T(8,128)(2,1)S(1)} %pad.8.v_ref), custom_call_target="tpu_custom_call" | custom-call | tf_op jit(solution)/shard_map/attend_head/pallas_call | solution.py:267
  84.8 0.0 copy-start
  84.8 0.8 copy-done
  85.6 31.5 %exchange_context.1 = bf16[16,128,64]{2,1,0:T(8,128)(2,1)} custom-call(bf16[16,128,64]{2,1,0:T(8,128)(2,1)} %copy-done), custom_call_target="tpu_custom_call" | custom-call | tf_op jit(solution)/shard_map/exchange_context/pallas_call | solution.py:307
  117.1 1.3 copy.21
  119.0 0.7 add_compare_fusion.1
  119.7 0.7 fusion.24.valid_ref
  120.3 0.0 all-gather.3.cloned.1.call-done
  120.4 2.2 %convert_reduce_fusion = (f32[128]{0:T(128)S(1)}, bf16[128,1024]{1,0:T(8,128)(2,1)S(1)}) fusion(bf16[128,1024]{0,1:T(8,128)(2,1)S(1)} %bitcast.40, bf16[1024,1024]{1,0:T(8,128)(2,1)} %all-gather.3.cloned.1.call-done, bf16[1,128,1024]{2,1,0:T(8,128)(2,1)S(1)} %copy-done.4, pred[128]{0:T(512)(128)(4,1)S(1)} %add_compare_fusion.1), kind=kOutput, calls=%fused_computation.5 | convolution fusion | flops 269221760 | bytes 2884224 | tf_op jit(solution)/shard_map/dot_general | solution.py:47
  122.5 0.0 copy-start.5
  122.5 0.0 copy-start.1
  122.5 0.0 copy-start.2
  122.6 0.0 copy-start.3
  122.6 0.2 fusion.7
  122.8 8.9 %all-gather.5.cloned.1.call-done = bf16[1024,2048]{1,0:T(8,128)(2,1)} async-done(((bf16[64,2048]{1,0:T(8,128)(2,1)}), bf16[1024,2048]{1,0:T(8,128)(2,1)}) %all-gather.5.cloned.1.call-update) | async-done | bytes 4194320 | tf_op jit(solution)/shard_map/all_gather | solution.py:460
  131.7 0.0 copy-done.7
  131.7 3.0 %fusion.19 = f32[128,2048]{1,0:T(8,128)S(1)} fusion(bf16[1024,2048]{1,0:T(8,128)(2,1)} %all-gather.5.cloned.1.call-done, bf16[128,1024]{1,0:T(8,128)(2,1)S(1)} %get-tuple-element.10, f32[1024]{0:T(1024)S(1)} %copy-done.7, f32[128]{0:T(128)S(1)} %add_rsqrt_fusion, f32[128]{0:T(128)S(1)} %broadcast_multiply_fusion), kind=kOutput, calls=%fused_computation.26 | convolution fusion | flops 537526272 | bytes 5510144 | tf_op jit(solution)/shard_map/dot_general | solution.py:47
  134.7 0.2 fusion.18.g_ref
  134.9 0.0 copy-done.1
  134.9 0.0 copy-done.2
  134.9 0.0 copy-done.3
  134.9 13.6 %conv_norm.1 = bf16[128,1024]{1,0:T(8,128)(2,1)S(1)} custom-call(bf16[128,1024]{1,0:T(8,128)(2,1)S(1)} %fusion.18.g_ref, f32[128,1]{1,0:T(8,128)S(1)} %fusion.24.valid_ref, f32[1,1]{1,0:T(1,128)} %bitcast.9.total_ref, f32[9,1024]{1,0:T(8,128)S(1)} %copy-done.1, f32[1,1024]{1,0:T(1,128)S(1)} %bitcast.35, f32[1,1024]{1,0:T(1,128)S(1)} %bitcast.36), custom_call_target="tpu_custom_call" | custom-call | tf_op jit(solution)/shard_map/conv_norm/pallas_call | solution.py:411
  148.5 0.7 copy.25
  149.2 0.0 copy-done.5
  (4 shorter events, 0.0 us)
Async XLA Ops:
  7.2 7.6 %copy-start.4 = (bf16[1,128,1024]{2,1,0:T(8,128)(2,1)S(1)}, bf16[1,128,1024]{2,1,0:T(8,128)(2,1)}, u32[]{:S(2)}) copy-start(bf16[1,128,1024]{2,1,0:T(8,128)(2,1)} %param.10) | copy-start | bytes 786436
  7.2 8.0 %copy-start.6 = (f32[1024]{0:T(1024)S(1)}, f32[1024]{0:T(1024)}, u32[]{:S(2)}) copy-start(f32[1024]{0:T(1024)} %param.12) | copy-start | bytes 12292
  7.2 113.2 %all-gather.3.cloned.1.call-start = ((), (), s32[]{:S(2)}) async-start(), calls=%async_computation | async-start | bytes 2228224 | tf_op jit(solution)/shard_map/all_gather | solution.py:455
  7.9 123.8 %all-gather.5.cloned.1.call-start = ((), (), s32[]{:S(2)}) async-start(), calls=%async_computation.1 | async-start | bytes 4456448 | tf_op jit(solution)/shard_map/all_gather | solution.py:460
  74.4 57.3 %copy-start.7 = (f32[1024]{0:T(1024)S(1)}, f32[1024]{0:T(1024)}, u32[]{:S(2)}) copy-start(f32[1024]{0:T(1024)} %param.15) | copy-start | bytes 12292
  84.8 0.8 copy-start
  122.5 26.7 %copy-start.5 = (bf16[128,1024]{1,0:T(8,128)(2,1)}, bf16[128,1024]{1,0:T(8,128)(2,1)S(1)}, u32[]{:S(2)}) copy-start(bf16[128,1024]{1,0:T(8,128)(2,1)S(1)} %get-tuple-element.10) | copy-start | bytes 786436
  122.5 12.3 %copy-start.1 = (f32[9,1024]{1,0:T(8,128)S(1)}, f32[9,1024]{1,0:T(8,128)}, u32[]{:S(2)}) copy-start(f32[9,1024]{1,0:T(8,128)} %taps_ref.1) | copy-start | bytes 110596
  122.5 12.3 %copy-start.2 = (f32[1024]{0:T(1024)S(1)}, f32[1024]{0:T(1024)}, u32[]{:S(2)}) copy-start(f32[1024]{0:T(1024)} %param.18) | copy-start | bytes 12292
  122.6 12.3 %copy-start.3 = (f32[1024]{0:T(1024)S(1)}, f32[1024]{0:T(1024)}, u32[]{:S(2)}) copy-start(f32[1024]{0:T(1024)} %param.19) | copy-start | bytes 12292
Sparse Core Ops, SparseCore 0:
  10.2 62.5 all-gather.2
  74.9 56.7 all-gather.4

commit v2 on v1

--- a/solution.py
+++ b/solution.py
@@ -156,11 +156,22 @@
     pl.semaphore_wait(barrier, len(places))
 
 
-def gather_kernel(count, x_ref, w_ref, xall, wcol, send_x, recv_x, send_w, recv_w, own_sem):
+def gather_kernel(
+    count, stream_ref, gain_ref, rows_ref, xall, wcol, x_ref, w_ref,
+    send_x, recv_x, send_w, recv_w, own_sem,
+):
     me = lax.axis_index("tm")
     y_peer = me + 2 - 4 * ((me // 2) % 2)
     c_peer = me + 1 - 2 * (me % 2)
     both = y_peer + 1 - 2 * (me % 2)
+    x_ref[...] = layer_norm(stream_ref[...], gain_ref[...]).astype(jnp.bfloat16)
+    width = rows_ref.shape[1] // 3
+    for head in range(count):
+        for part in range(3):
+            start = part * width + head * HEAD_DIM
+            w_ref[head, :, part * HEAD_DIM : (part + 1) * HEAD_DIM] = rows_ref[
+                :, start : start + HEAD_DIM
+            ]
     greet([{"tm": (me + step) % count} for step in range(1, count)])
     own_x = pltpu.make_async_copy(x_ref, xall.at[me], own_sem.at[0])
     own_w = pltpu.make_async_copy(w_ref.at[me], wcol.at[me], own_sem.at[1])
@@ -220,103 +231,190 @@
     own_w.wait()
 
 
-def gather_call(normed, w_heads):
-    count = w_heads.shape[0]
+def gather_call(stream, gain, w_rows):
+    count = lax.axis_size("tm")
+    depth = w_rows.shape[0]
+    heads = (count, depth, 3 * HEAD_DIM)
     anywhere = pl.BlockSpec(memory_space=pl.ANY)
+    vmem = pl.BlockSpec(memory_space=pltpu.VMEM)
+    sems = pltpu.SemaphoreType.DMA
     return pl.pallas_call(
         functools.partial(gather_kernel, count),
         out_shape=(
-            jax.ShapeDtypeStruct((count,) + normed.shape, normed.dtype),
-            jax.ShapeDtypeStruct(w_heads.shape, w_heads.dtype),
+            jax.ShapeDtypeStruct((count,) + stream.shape, jnp.bfloat16),
+            jax.ShapeDtypeStruct(heads, jnp.bfloat16),
         ),
-        in_specs=[anywhere] * 2,
+        in_specs=[vmem] * 3,
         out_specs=(anywhere, anywhere),
         scratch_shapes=[
-            pltpu.SemaphoreType.DMA((count,)),
-            pltpu.SemaphoreType.DMA((count,)),
-            pltpu.SemaphoreType.DMA((count,)),
-            pltpu.SemaphoreType.DMA((count,)),
-            pltpu.SemaphoreType.DMA((2,)),
+            pltpu.VMEM(stream.shape, jnp.bfloat16),
+            pltpu.VMEM(heads, jnp.bfloat16),
+            sems((count,)), sems((count,)), sems((count,)), sems((count,)), sems((2,)),
         ],
-        compiler_params=pltpu.CompilerParams(collective_id=0, has_side_effects=True),
+        compiler_params=pltpu.CompilerParams(
+            collective_id=0, has_side_effects=True, vmem_limit_bytes=24 * 1024 * 1024
+        ),
         name="gather_frames",
-    )(normed, w_heads)
-
-
-def attend_kernel(scale, length_ref, q_ref, k_ref, v_ref, out_ref):
-    block = pl.program_id(0)
-    width = LEFT + SPAN
-    first = pl.multiple_of(block * SPAN, SPAN)
-    keys = k_ref[pl.ds(first, width), :]
-    scores = lax.dot_general(
-        q_ref[...], keys, (((1,), (1,)), ((), ())), preferred_element_type=jnp.float32
-    )
-    key_pos = block * SPAN - LEFT + lax.broadcasted_iota(jnp.int32, (SPAN, width), 1)
-    query_pos = block * SPAN + lax.broadcasted_iota(jnp.int32, (SPAN, width), 0)
-    allowed = (key_pos >= 0) & ((key_pos < length_ref[0]) | (key_pos == query_pos))
-    raised = jnp.where(allowed, jnp.exp(scores * scale), 0.0)
-    probs = (raised / jnp.sum(raised, axis=-1, keepdims=True)).astype(jnp.bfloat16)
-    mixed = jnp.dot(probs, v_ref[pl.ds(first, width), :], preferred_element_type=jnp.float32)
-    out_ref[0] = mixed.astype(jnp.bfloat16)
-
-
-def attend_call(length, queries, keys, values):
-    frames, width = queries.shape
-    count = frames // SPAN
-    whole = pl.BlockSpec((frames + LEFT, width), lambda i: (0, 0))
-    return pl.pallas_call(
-        functools.partial(attend_kernel, HEAD_DIM**-0.5),
-        grid=(count,),
-        out_shape=jax.ShapeDtypeStruct((count, SPAN, width), jnp.bfloat16),
-        in_specs=[
-            pl.BlockSpec(memory_space=pltpu.SMEM),
-            pl.BlockSpec((SPAN, width), lambda i: (i, 0)),
-            whole,
-            whole,
-        ],
-        out_specs=pl.BlockSpec((1, SPAN, width), lambda i: (i, 0, 0)),
-        compiler_params=pltpu.CompilerParams(vmem_limit_bytes=32 * 1024 * 1024),
-        name="attend_head",
-    )(length, queries, keys, values)
-
-
-def exchange_kernel(count, x_ref, out_ref, send, recv, own_sem):
+    )(stream, gain, w_rows)
+
+
+def attend_kernel(
+    count, scale, length_ref, q_ref, k_ref, v_ref, rows_ref, out_ref, wall,
+    mixed_ref, landed, send_c, recv_c, send_w, recv_w, own_sem,
+):
     me = lax.axis_index("tm")
-    greet([{"tm": (me + step) % count} for step in range(1, count)])
-    own = pltpu.make_async_copy(x_ref.at[me], out_ref.at[me], own_sem.at[0])
-    own.start()
+    call = lax.axis_index("call")
+    y_peer = me + 2 - 4 * ((me // 2) % 2)
+    c_peer = me + 1 - 2 * (me % 2)
+    twin = {"call": 1 - call, "tm": me}
+    greet([{"tm": (me + step) % count} for step in range(1, count)] + [twin])
     sends = []
-    for step in range(1, count):
-        place = (me + step) % count
-        copy = remote(x_ref.at[place], out_ref.at[me], send.at[step], recv.at[me], {"tm": place})
+
+    def push(source, part, owner, where):
+        copy = remote(
+            source, wall.at[part, owner], send_w.at[len(sends)], recv_w.at[part, owner], where
+        )
         copy.start()
         sends.append(copy)
+
+    def arrived(part, owner):
+        remote(
+            wall.at[part, owner], wall.at[part, owner], send_w.at[0], recv_w.at[part, owner],
+            {"tm": c_peer},
+        ).wait_recv()
+
+    def relay(part, owner, places):
+        arrived(part, owner)
+        for where in places:
+            push(wall.at[part, owner], part, owner, where)
+
+    width = LEFT + SPAN
+    length = length_ref[call]
+
+    def attend(block):
+        first = pl.multiple_of(block * SPAN, SPAN)
+        scores = lax.dot_general(
+            q_ref[pl.ds(first, SPAN), :],
+            k_ref[pl.ds(first, width), :],
+            (((1,), (1,)), ((), ())),
+            preferred_element_type=jnp.float32,
+        )
+        key_pos = block * SPAN - LEFT + lax.broadcasted_iota(jnp.int32, (SPAN, width), 1)
+        query_pos = block * SPAN + lax.broadcasted_iota(jnp.int32, (SPAN, width), 0)
+        allowed = (key_pos >= 0) & ((key_pos < length) | (key_pos == query_pos))
+        raised = jnp.where(allowed, jnp.exp(scores * scale), 0.0)
+        probs = (raised / jnp.sum(raised, axis=-1, keepdims=True)).astype(jnp.bfloat16)
+        mixed = jnp.dot(probs, v_ref[pl.ds(first, width), :], preferred_element_type=jnp.float32)
+        return mixed.astype(jnp.bfloat16)
+
+    def attend_and_send(step, carry):
+        place = (me + step) % count
+        mixed_ref[place] = attend(place)
+        remote(
+            mixed_ref.at[place], landed.at[me], send_c.at[place], recv_c.at[me], {"tm": place}
+        ).start()
+        return carry
+
+    hops = range(4, count, 4)
+    own = pltpu.make_async_copy(rows_ref, wall.at[:, me], own_sem.at[0])
+    own.start()
+    for hop in hops:
+        for part in (call, 2):
+            push(rows_ref.at[part], part, me, {"tm": (me + hop) % count})
+    for part in (call, 2):
+        push(rows_ref.at[part], part, me, {"tm": y_peer})
+    for part in range(3):
+        push(rows_ref.at[part], part, me, {"tm": c_peer})
+    lax.fori_loop(1, count // 2, attend_and_send, 0)
+    relay(call, y_peer, [twin, {"tm": c_peer}])
+    relay(2, y_peer, [{"tm": c_peer}])
+    relay(call, (me + 4) % count, [{"tm": y_peer}, twin, {"tm": c_peer}])
+    relay(2, (me + 4) % count, [{"tm": y_peer}, {"tm": c_peer}])
+    lax.fori_loop(count // 2, count, attend_and_send, 0)
+    landed[me] = attend(me)
+    for hop in range(8, count, 4):
+        owner = (me + hop) % count
+        relay(call, owner, [{"tm": y_peer}, twin, {"tm": c_peer}])
+        relay(2, owner, [{"tm": y_peer}, {"tm": c_peer}])
+    for hop in hops:
+        owner = (y_peer + hop) % count
+        relay(call, owner, [twin, {"tm": c_peer}])
+        relay(2, owner, [{"tm": c_peer}])
+    relay(1 - call, y_peer, [{"tm": c_peer}])
+    for hop in hops:
+        relay(1 - call, (me + hop) % count, [{"tm": c_peer}])
+        relay(1 - call, (y_peer + hop) % count, [{"tm": c_peer}])
     for step in range(1, count):
         owner = (me + step) % count
         remote(
-            x_ref.at[owner], out_ref.at[owner], send.at[0], recv.at[owner], {"tm": owner}
-        ).wait_recv()
+            mixed_ref.at[owner], landed.at[owner], send_c.at[owner], recv_c.at[owner],
+            {"tm": owner},
+        ).wait()
+    for pair in range(0, count, 2):
+        out_ref[:, pair * HEAD_DIM : (pair + 2) * HEAD_DIM] = jnp.concatenate(
+            [landed[pair], landed[pair + 1]], axis=1
+        )
+    own.wait()
+    both = c_peer + 2 - 4 * ((me // 2) % 2)
+    for part in range(3):
+        for hop in range(0, count, 4):
+            arrived(part, (c_peer + hop) % count)
+            arrived(part, (both + hop) % count)
     for copy in sends:
         copy.wait_send()
-    own.wait()
-
-
-def exchange_call(blocks):
-    count = blocks.shape[0]
+
+
+def attend_call(lengths, queries, keys, values, rows):
+    frames, width = queries.shape
+    count = frames // SPAN
     anywhere = pl.BlockSpec(memory_space=pl.ANY)
+    vmem = pl.BlockSpec(memory_space=pltpu.VMEM)
+    sems = pltpu.SemaphoreType.DMA
+    parts, depth, columns = rows.shape
+    copies = 2 * (count // 4 - 1) + 5 + 3 + 5 * (count // 4 - 1) + 3 * (count // 4 - 1) + 7
     return pl.pallas_call(
-        functools.partial(exchange_kernel, count),
-        out_shape=jax.ShapeDtypeStruct(blocks.shape, blocks.dtype),
-        in_specs=[anywhere],
-        out_specs=anywhere,
+        functools.partial(attend_kernel, count, HEAD_DIM**-0.5),
+        out_shape=(
+            jax.ShapeDtypeStruct((SPAN, count * width), jnp.bfloat16),
+            jax.ShapeDtypeStruct((parts, count, depth, columns), jnp.bfloat16),
+        ),
+        in_specs=[pl.BlockSpec(memory_space=pltpu.SMEM), vmem, vmem, vmem, anywhere],
+        out_specs=(vmem, anywhere),
         scratch_shapes=[
-            pltpu.SemaphoreType.DMA((count,)),
-            pltpu.SemaphoreType.DMA((count,)),
-            pltpu.SemaphoreType.DMA((1,)),
+            pltpu.VMEM((count, SPAN, width), jnp.bfloat16),
+            pltpu.VMEM((count, SPAN, width), jnp.bfloat16),
+            sems((count,)), sems((count,)), sems((copies,)), sems((parts, count)), sems((1,)),
         ],
-        compiler_params=pltpu.CompilerParams(collective_id=1, has_side_effects=True),
-        name="exchange_context",
-    )(blocks)
+        compiler_params=pltpu.CompilerParams(
+            collective_id=1, has_side_effects=True, vmem_limit_bytes=32 * 1024 * 1024
+        ),
+        name="attend_exchange",
+    )(lengths, queries, keys, values, rows)
+
+
+def project_kernel(length_ref, context_ref, stream_ref, w_ref, gain_ref, attended_ref, gated_ref):
+    rows = stream_ref.shape[0]
+    first = lax.axis_index("tm") * rows
+    length = length_ref[lax.axis_index("call")]
+    valid = first + lax.broadcasted_iota(jnp.int32, (rows, 1), 0) < length
+    wide = stream_ref[...].astype(jnp.float32) + contract_with(context_ref[...], w_ref[0])
+    attended = jnp.where(valid, wide, 0.0).astype(jnp.bfloat16)
+    attended_ref[...] = attended
+    conv_in = layer_norm(attended, gain_ref[...]).astype(jnp.bfloat16)
+    gated = contract_with(conv_in, w_ref[1]) * jax.nn.sigmoid(contract_with(conv_in, w_ref[2]))
+    gated_ref[...] = jnp.where(valid, gated, 0.0).astype(jnp.bfloat16)
+
+
+def project_call(lengths, context, stream, weights, gain):
+    vmem = pl.BlockSpec(memory_space=pltpu.VMEM)
+    return pl.pallas_call(
+        project_kernel,
+        out_shape=(jax.ShapeDtypeStruct(stream.shape, jnp.bfloat16),) * 2,
+        in_specs=[pl.BlockSpec(memory_space=pltpu.SMEM)] + [vmem] * 4,
+        out_specs=(vmem, vmem),
+        compiler_params=pltpu.CompilerParams(vmem_limit_bytes=32 * 1024 * 1024),
+        name="project_gate",
+    )(lengths, context, stream, weights, gain)
 
 
 EDGE = 16
@@ -324,7 +422,7 @@
 
 
 def conv_kernel(
-    count, g_ref, valid_ref, total_ref, taps_ref, gain_ref, bias_ref, out_ref,
+    count, length_ref, g_ref, taps_ref, gain_ref, bias_ref, out_ref,
     low, high, padded, depth, mine, plane, near, far,
     halo_send, halo_recv, near_send, near_recv, far_send, far_recv,
 ):
@@ -359,7 +457,8 @@
     has_high = jnp.where(me < count - 1, 1.0, 0.0).astype(jnp.float32)
     padded[0:EDGE, :] = low[...].astype(jnp.float32) * has_low
     padded[EDGE + rows : 2 * EDGE + rows, :] = high[...].astype(jnp.float32) * has_high
-    valid = valid_ref[...]
+    first = me * rows + lax.broadcasted_iota(jnp.int32, (rows, 1), 0)
+    valid = jnp.where(first < length_ref[call], 1.0, 0.0).astype(jnp.float32)
     for at in range(0, width, STRIP):
         strip = slice(at, at + STRIP)
         total = jnp.zeros((rows, STRIP), jnp.float32)
@@ -390,7 +489,7 @@
         copy.wait_recv()
     for slot in range(len(hops)):
         both = both + far[slot]
-    both = both / total_ref[...]
+    both = both / (length_ref[0] + length_ref[1]).astype(jnp.float32)
     average = both[0:1]
     spread = lax.rsqrt(both[1:2] - average * average + 1e-05)
     for at in range(0, width, STRIP):
@@ -403,7 +502,7 @@
         copy.wait_send()
 
 
-def conv_call(count, gated, valid, total, taps, gain, bias):
+def conv_call(count, lengths, gated, taps, gain, bias):
     rows, width = gated.shape
     vmem = pl.BlockSpec(memory_space=pltpu.VMEM)
     sems = pltpu.SemaphoreType.DMA
@@ -411,7 +510,7 @@
     return pl.pallas_call(
         functools.partial(conv_kernel, count),
         out_shape=jax.ShapeDtypeStruct(gated.shape, jnp.bfloat16),
-        in_specs=[vmem] * 6,
+        in_specs=[pl.BlockSpec(memory_space=pltpu.SMEM)] + [vmem] * 4,
         out_specs=vmem,
         scratch_shapes=[
             pltpu.VMEM((EDGE, width), jnp.bfloat16),
@@ -428,47 +527,27 @@
             collective_id=2, has_side_effects=True, vmem_limit_bytes=32 * 1024 * 1024
         ),
         name="conv_norm",
-    )(gated, valid, total, taps, gain, bias)
+    )(lengths, gated, taps, gain, bias)
 
 
 def one_head_each(
     frames, lengths, ln_attn_gain, w_qkv, w_out, ln_conv_gain, w_pw1, dw_kernel, bn_gain, bn_bias
 ):
     stream = frames[0]
-    frame_count, model_width = stream.shape
+    model_width = stream.shape[1]
     count = lax.axis_size("tm")
-    length = lax.dynamic_index_in_dim(lengths, lax.axis_index("call"), 0, keepdims=False)
-    query_pos = lax.axis_index("tm") * frame_count + jnp.arange(frame_count, dtype=jnp.int32)
-    frame_valid = (query_pos < length)[:, None]
-    normed = layer_norm(stream, ln_attn_gain).astype(jnp.bfloat16)
-    w_heads = w_qkv.reshape(-1, 3, count, HEAD_DIM).transpose(2, 0, 1, 3)
-    w_heads = w_heads.reshape(count, -1, 3 * HEAD_DIM)
-    all_frames, w_columns = gather_call(normed, w_heads)
+    all_frames, w_columns = gather_call(stream, ln_attn_gain[None], w_qkv)
     packed = contract_with(
         all_frames.reshape(-1, model_width), w_columns.reshape(model_width, -1)
     ).astype(jnp.bfloat16)
     queries = packed[:, :HEAD_DIM]
     keys = jnp.pad(packed[:, HEAD_DIM : 2 * HEAD_DIM], ((LEFT, 0), (0, 0)))
     values = jnp.pad(packed[:, 2 * HEAD_DIM :], ((LEFT, 0), (0, 0)))
-    blocks = attend_call(length[None], queries, keys, values)
-    context = exchange_call(blocks).transpose(1, 0, 2).reshape(frame_count, model_width)
-    projected = contract_with(context, lax.all_gather(w_out, "tm", axis=0, tiled=True))
-    attended = jnp.where(frame_valid, stream.astype(jnp.float32) + projected, 0.0).astype(
-        jnp.bfloat16
-    )
-    conv_in = layer_norm(attended, ln_conv_gain).astype(jnp.bfloat16)
-    expanded = contract_with(conv_in, lax.all_gather(w_pw1, "tm", axis=0, tiled=True))
-    gated = expanded[:, :model_width] * jax.nn.sigmoid(expanded[:, model_width:])
-    gated = jnp.where(frame_valid, gated, 0.0).astype(jnp.bfloat16)
-    conv_act = conv_call(
-        count,
-        gated,
-        frame_valid.astype(jnp.float32),
-        jnp.sum(lengths).astype(jnp.float32).reshape(1, 1),
-        dw_kernel,
-        bn_gain[None],
-        bn_bias[None],
-    )
+    rows = jnp.stack([w_out, w_pw1[:, :model_width], w_pw1[:, model_width:]])
+    context, weights = attend_call(lengths, queries, keys, values, rows)
+    weights = weights.reshape(3, model_width, model_width)
+    attended, gated = project_call(lengths, context, stream, weights, ln_conv_gain[None])
+    conv_act = conv_call(count, lengths, gated, dw_kernel, bn_gain[None], bn_bias[None])
     return (attended[None], conv_act[None])
 
 

time: 156 us -> 136 us (0.87)
  Pallas kernels: 110 us -> 128 us
  between operations: 14.9 us -> 0.8 us
  waiting for transfers between devices: 10.3 us -> 0 us
  matrix products: 8.82 us -> 1.28 us
  other arithmetic: 4.34 us -> 0.95 us
  local copies, waits for them, and re-layouts: 8.09 us -> 4.95 us
    pallas_call x2, Pallas kernels: 41.7 us -> 58.3 us  [the longest x1 56.4 us: attend_call(): pl.pallas_call(functools.partial(attend_kernel, count, HEAD_DIM ** (-0.5)...]
    pallas_call x1, Pallas kernels: 13.6 us -> 26.1 us  [conv_call(): pl.pallas_call(functools.partial(conv_kernel, count), out_shape=jax.Shape...]
    pallas_call x1, Pallas kernels: 54.2 us -> 43.8 us  [gather_call(): pl.pallas_call(functools.partial(gather_kernel, count), out_shape=(jax.Sh...]
    all_gather x2 -> x0, waiting for transfers between devices: 8.93 us -> none  [the longest x1 8.91 us: one_head_each(): lax.all_gather(w_pw1, 'tm', axis=0, tiled=True)]
    dot_general x3 -> x1, matrix products: 8.82 us -> 1.28 us  [contract_with(): return jnp.dot(left, rows_piece, preferred_element_type=jnp.float32)]
    reshape x3 -> x0, local copies, waits for them, and re-layouts: 3.48 us -> none  [the longest x2 2.32 us: one_head_each(): w_heads = w_qkv.reshape(-1, 3, count, HEAD_DIM).transpose(2, 0, 1, 3)]
    reduce_sum x4 -> x0, other arithmetic: 1.91 us -> none  [the longest x1 1.36 us: one_head_each(): jnp.sum(lengths).astype(jnp.float32).reshape(1, 1)]
    unnamed x17 -> x19, local copies, waits for them, and re-layouts: 1.53 us -> 3.37 us
  transfers between devices with their start and end apart: 2 -> 0, of which waited for: 1 -> 0; matrix products, arithmetic and copies ran while one was open for 11% -> 0% of each run, Pallas kernels for 61% -> 0%
where the time goes in v2:
time: 136 us
  Pallas kernels  128 us (94%)
  local copies, waits for them, and re-layouts  4.95 us (4%)
    pallas_call x1, Pallas kernels, attend_call(): pl.pallas_call(functools.partial(attend_kernel, count, HEAD_DIM ** (-0.5)...  56.4 us
    pallas_call x1, Pallas kernels, gather_call(): pl.pallas_call(functools.partial(gather_kernel, count), out_shape=(jax.Sh...  43.8 us
    pallas_call x1, Pallas kernels, conv_call(): pl.pallas_call(functools.partial(conv_kernel, count), out_shape=jax.Shape...  26.1 us
    unnamed x19, local copies, waits for them, and re-layouts  3.37 us

profile of v2, /device:TPU:0, one launch (start us, length us, event | category | flops | bytes accessed | tf_op | source)
XLA Modules:
  0.0 136.2 jit_solution(10699066711666645200)
XLA Ops:
  0.6 1.0 slice_bitcast_fusion.1
  1.6 1.0 pad_maximum_fusion.rows_ref
  2.6 0.0 copy-start
  2.6 0.9 copy-done
  3.5 0.0 copy-start.2
  3.5 1.0 copy-done.2
  4.5 0.0 copy-start.5
  4.5 0.7 copy-done.5
  5.2 43.8 %gather_frames.1 = (bf16[16,128,1024]{2,1,0:T(8,128)(2,1)S(1)}, bf16[16,64,192]{2,1,0:T(8,128)(2,1)S(1)}) custom-call(bf16[128,1024]{1,0:T(8,128)(2,1)S(1)} %bitcast.18, f32[1,1024]{1,0:T(1,128)S(1)} %bitcast.21, bf16[64,3072]{1,0:T(8,128)(2,1)S(1)} %copy-done.2), custom_call_target="tpu_custom_call" | custom-call | tf_op jit(solution)/shard_map/gather_frames/pallas_call | solution.py:241
  49.0 1.3 convolution_convert_fusion
  50.3 0.0 copy-start.4
  50.3 0.0 copy-start.1
  50.4 0.0 copy-start.6
  50.4 0.3 fusion
  50.7 0.1 pad.8.v_ref
  50.8 0.1 pad.7.k_ref
  51.0 0.0 copy-done.4
  51.0 0.0 copy-start.3
  51.0 0.0 copy-start.7
  51.0 0.0 copy-start.8
  51.0 56.4 %attend_exchange.1 = (bf16[128,1024]{1,0:T(8,128)(2,1)S(1)}, bf16[3,16,64,1024]{3,2,1,0:T(8,128)(2,1)S(1)}) custom-call(s32[2]{0:T(128)S(1)} %copy-done.4, bf16[2048,64]{1,0:T(8,128)(2,1)S(1)} %get-tuple-element.16.q_ref, bf16[3072,64]{1,0:T(8,128)(2,1)S(1)} %pad.7.k_ref, bf16[3072,64]{1,0:T(8,128)(2,1)S(1)} %pad.8.v_ref, ...), custom_call_target="tpu_custom_call" | custom-call | tf_op jit(solution)/shard_map/attend_exchange/pallas_call | solution.py:375
  107.4 0.0 copy-done.1
  107.4 0.0 copy-done.6
  107.4 1.9 %project_gate.1 = (bf16[128,1024]{1,0:T(8,128)(2,1)}, bf16[128,1024]{1,0:T(8,128)(2,1)S(1)}) custom-call(s32[2]{0:T(128)S(1)} %copy-done.4, bf16[128,1024]{1,0:T(8,128)(2,1)S(1)} %get-tuple-element.10.context_ref, bf16[128,1024]{1,0:T(8,128)(2,1)S(1)} %bitcast.19, bf16[3,1024,1024]{2,1,0:T(8,128)(2,1)S(1)} %bitcast.17, f32[1,1024]{1,0:T(1,128)S(1)} %bitcast.22), custom_call_target="tpu_custom_call" | custom-call | tf_op jit(solution)/shard_map/project_gate/pallas_call | solution.py:410
  109.4 0.0 copy-done.3
  109.4 0.0 copy-done.7
  109.4 0.0 copy-done.8
  109.4 26.1 %conv_norm.1 = bf16[128,1024]{1,0:T(8,128)(2,1)S(1)} custom-call(s32[2]{0:T(128)S(1)} %copy-done.4, bf16[128,1024]{1,0:T(8,128)(2,1)S(1)} %get-tuple-element.13.g_ref, f32[9,1024]{1,0:T(8,128)S(1)} %copy-done.3, f32[1,1024]{1,0:T(1,128)S(1)} %bitcast.23, f32[1,1024]{1,0:T(1,128)S(1)} %bitcast.24), custom_call_target="tpu_custom_call" | custom-call | tf_op jit(solution)/shard_map/conv_norm/pallas_call | solution.py:510
  135.5 0.7 copy.15
Async XLA Ops:
  2.6 1.0 copy-start
  3.5 1.0 copy-start.2
  4.5 0.7 copy-start.5
  50.3 0.7 copy-start.4
  50.3 57.1 %copy-start.1 = (bf16[1,128,1024]{2,1,0:T(8,128)(2,1)S(1)}, bf16[1,128,1024]{2,1,0:T(8,128)(2,1)}, u32[]{:S(2)}) copy-start(bf16[1,128,1024]{2,1,0:T(8,128)(2,1)} %param.10) | copy-start | bytes 786436
  50.4 57.1 %copy-start.6 = (f32[1024]{0:T(1024)S(1)}, f32[1024]{0:T(1024)}, u32[]{:S(2)}) copy-start(f32[1024]{0:T(1024)} %param.15) | copy-start | bytes 12292
  51.0 58.4 %copy-start.3 = (f32[9,1024]{1,0:T(8,128)S(1)}, f32[9,1024]{1,0:T(8,128)}, u32[]{:S(2)}) copy-start(f32[9,1024]{1,0:T(8,128)} %taps_ref.1) | copy-start | bytes 110596
  51.0 58.4 %copy-start.7 = (f32[1024]{0:T(1024)S(1)}, f32[1024]{0:T(1024)}, u32[]{:S(2)}) copy-start(f32[1024]{0:T(1024)} %param.18) | copy-start | bytes 12292
  51.0 58.4 %copy-start.8 = (f32[1024]{0:T(1024)S(1)}, f32[1024]{0:T(1024)}, u32[]{:S(2)}) copy-start(f32[1024]{0:T(1024)} %param.19) | copy-start | bytes 12292

commit v3 on v2

--- a/solution.py
+++ b/solution.py
@@ -156,15 +156,152 @@
     pl.semaphore_wait(barrier, len(places))
 
 
+class Relay:
+    def __init__(self, count, buffer, sems):
+        self.count = count
+        self.buffer = buffer
+        self.up, self.down, self.over, self.across, self.landed = sems
+        self.me = lax.axis_index("tm")
+        self.planes = count // 4
+        self.plane = self.me // 4
+        self.y_peer = self.me + 2 - 4 * ((self.me // 2) % 2)
+        self.c_peer = self.me + 1 - 2 * (self.me % 2)
+
+    def copy(self, source, part, owner, send, place):
+        return remote(
+            source,
+            self.buffer.at[part, owner],
+            send.at[part, owner],
+            self.landed.at[part, owner],
+            {"tm": place % self.count},
+        )
+
+    def held(self, part, owner):
+        return self.buffer.at[part, owner]
+
+    def arrived(self, part, owner):
+        self.copy(self.held(part, owner), part, owner, self.across, self.c_peer).wait_recv()
+
+    def start(self, source, part):
+        me = self.me
+
+        @pl.when(self.plane < self.planes - 1)
+        def _():
+            self.copy(source, part, me, self.up, me + 4).start()
+
+        @pl.when(self.plane > 0)
+        def _():
+            self.copy(source, part, me, self.down, me + self.count - 4).start()
+
+        self.copy(source, part, me, self.over, self.y_peer).start()
+
+    def start_across(self, source, part):
+        self.copy(source, part, self.me, self.across, self.c_peer).start()
+
+    def step(self, at, part, extra=None):
+        me = self.me
+        far = 4 * (at + 1)
+
+        @pl.when(self.plane > at)
+        def _():
+            owner = me - far
+            self.arrived(part, owner)
+            held = self.held(part, owner)
+
+            @pl.when(self.plane < self.planes - 1)
+            def _():
+                self.copy(held, part, owner, self.up, me + 4).start()
+
+            self.copy(held, part, owner, self.over, self.y_peer).start()
+            if extra is not None:
+                extra(part, owner)
+            self.copy(held, part, owner, self.across, self.c_peer).start()
+
+        @pl.when(self.plane + at + 1 < self.planes)
+        def _():
+            owner = me + far
+            self.arrived(part, owner)
+            held = self.held(part, owner)
+
+            @pl.when(self.plane > 0)
+            def _():
+                self.copy(held, part, owner, self.down, me + self.count - 4).start()
+
+            self.copy(held, part, owner, self.over, self.y_peer).start()
+            if extra is not None:
+                extra(part, owner)
+            self.copy(held, part, owner, self.across, self.c_peer).start()
+
+    def pass_across(self, part, owner, extra=None):
+        self.arrived(part, owner)
+        if extra is not None:
+            extra(part, owner)
+        self.copy(self.held(part, owner), part, owner, self.across, self.c_peer).start()
+
+    def step_over(self, at, part, extra=None):
+        if at < 0:
+            self.pass_across(part, self.y_peer, extra)
+            return
+        far = 4 * (at + 1)
+
+        @pl.when(self.plane > at)
+        def _():
+            self.pass_across(part, self.y_peer - far, extra)
+
+        @pl.when(self.plane + at + 1 < self.planes)
+        def _():
+            self.pass_across(part, self.y_peer + far, extra)
+
+    def column(self, base):
+        return [(base + hop) % self.count for hop in range(0, self.count, 4)]
+
+    def receive_across(self, part):
+        both = self.c_peer + self.y_peer - self.me
+        for owner in self.column(self.c_peer) + self.column(both):
+            self.arrived(part, owner)
+
+    def finish_sends(self, part):
+        me = self.me
+        for owner in self.column(me):
+            plane = owner // 4
+
+            @pl.when((plane <= self.plane) & (self.plane < self.planes - 1))
+            def _():
+                self.copy(self.held(part, owner), part, owner, self.up, me + 4).wait_send()
+
+            @pl.when((plane >= self.plane) & (self.plane > 0))
+            def _():
+                place = me + self.count - 4
+                self.copy(self.held(part, owner), part, owner, self.down, place).wait_send()
+
+            self.copy(self.held(part, owner), part, owner, self.over, self.y_peer).wait_send()
+        for owner in self.column(me) + self.column(self.y_peer):
+            self.copy(self.held(part, owner), part, owner, self.across, self.c_peer).wait_send()
+
+
+def relay_sems(parts, count):
+    return [pltpu.SemaphoreType.DMA((parts, count)) for _ in range(5)]
+
+
 def gather_kernel(
-    count, stream_ref, gain_ref, rows_ref, xall, wcol, x_ref, w_ref,
-    send_x, recv_x, send_w, recv_w, own_sem,
+    count, stream_any, gain_ref, rows_any, xall, wcol, stream_ref, rows_ref, x_ref, w_ref,
+    up, down, over, across, landed, send_w, recv_w, twin_w, own_sem,
 ):
     me = lax.axis_index("tm")
-    y_peer = me + 2 - 4 * ((me // 2) % 2)
-    c_peer = me + 1 - 2 * (me % 2)
-    both = y_peer + 1 - 2 * (me % 2)
+    call = lax.axis_index("call")
+    twin = {"call": 1 - call, "tm": me}
+    relay = Relay(count, xall, (up, down, over, across, landed))
+    get_stream = pltpu.make_async_copy(stream_any, stream_ref, own_sem.at[0])
+    get_rows = pltpu.make_async_copy(rows_any, rows_ref, own_sem.at[1])
+    get_stream.start()
+    get_rows.start()
+    barrier = pltpu.get_barrier_semaphore()
+    places = [{"tm": (me + step) % count} for step in range(1, count)] + [twin]
+    for where in places:
+        pl.semaphore_signal(barrier, inc=1, device_id=where, device_id_type=MESH)
+    get_stream.wait()
     x_ref[...] = layer_norm(stream_ref[...], gain_ref[...]).astype(jnp.bfloat16)
+    get_rows.wait()
     width = rows_ref.shape[1] // 3
     for head in range(count):
         for part in range(3):
@@ -172,61 +309,60 @@
             w_ref[head, :, part * HEAD_DIM : (part + 1) * HEAD_DIM] = rows_ref[
                 :, start : start + HEAD_DIM
             ]
-    greet([{"tm": (me + step) % count} for step in range(1, count)])
-    own_x = pltpu.make_async_copy(x_ref, xall.at[me], own_sem.at[0])
-    own_w = pltpu.make_async_copy(w_ref.at[me], wcol.at[me], own_sem.at[1])
+    own_x = pltpu.make_async_copy(x_ref, xall.at[0, me], own_sem.at[2])
+    own_w = pltpu.make_async_copy(w_ref.at[me], wcol.at[me], own_sem.at[3])
     own_x.start()
     own_w.start()
-    sends = []
-
-    def push(source, owner, place):
-        copy = remote(
-            source, xall.at[owner], send_x.at[len(sends)], recv_x.at[owner], {"tm": place}
+    pl.semaphore_wait(barrier, len(places))
+    relay.start(x_ref, 0)
+
+    def slice_to(place):
+        return remote(
+            w_ref.at[place], wcol.at[me], send_w.at[place], recv_w.at[me], {"tm": place}
         )
-        copy.start()
-        sends.append(copy)
-
-    def arrived(owner):
-        remote(
-            xall.at[owner], xall.at[owner], send_x.at[0], recv_x.at[owner], {"tm": c_peer}
-        ).wait_recv()
-
-    hops = range(4, count, 4)
-    push(x_ref, me, y_peer)
-    for hop in hops:
-        push(x_ref, me, (me + hop) % count)
-    push(x_ref, me, c_peer)
-    w_sends = []
-    for step in range(1, count):
-        place = (me + step) % count
-        copy = remote(
-            w_ref.at[place], wcol.at[me], send_w.at[step], recv_w.at[me], {"tm": place}
-        )
-        copy.start()
-        w_sends.append(copy)
-    arrived(y_peer)
-    push(xall.at[y_peer], y_peer, c_peer)
-    for hop in hops:
-        owner = (me + hop) % count
-        arrived(owner)
-        push(xall.at[owner], owner, y_peer)
-        push(xall.at[owner], owner, c_peer)
-    for hop in hops:
-        owner = (y_peer + hop) % count
-        arrived(owner)
-        push(xall.at[owner], owner, c_peer)
-    arrived(c_peer)
-    arrived(both)
-    for hop in hops:
-        arrived((c_peer + hop) % count)
-        arrived((both + hop) % count)
-    for step in range(1, count):
-        owner = (me + step) % count
-        remote(
-            w_ref.at[owner], wcol.at[owner], send_w.at[0], recv_w.at[owner], {"tm": c_peer}
-        ).wait_recv()
-    for copy in sends + w_sends:
-        copy.wait_send()
+
+    def slice_on(owner):
+        return remote(wcol.at[owner], wcol.at[owner], twin_w.at[owner], recv_w.at[owner], twin)
+
+    @pl.when(me % 2 == call)
+    def _():
+        for step in range(1, count):
+            slice_to((me + step) % count).start()
+
+    relay.start_across(x_ref, 0)
+    steps = count // 4 - 1
+    relay.step(0, 0)
+    relay.step_over(-1, 0)
+    for pair in range(count // 2):
+        owner = 2 * pair + call
+
+        @pl.when(owner != me)
+        def _():
+            slice_on(owner).wait_recv()
+            slice_on(owner).start()
+
+    for at in range(1, steps):
+        relay.step(at, 0)
+        relay.step_over(at - 1, 0)
+    relay.step_over(steps - 1, 0)
+    for pair in range(count // 2):
+        owner, other = 2 * pair + call, 2 * pair + 1 - call
+
+        @pl.when(other != me)
+        def _():
+            slice_on(other).wait_recv()
+
+        @pl.when(owner != me)
+        def _():
+            slice_on(owner).wait_send()
+
+    @pl.when(me % 2 == call)
+    def _():
+        for step in range(1, count):
+            slice_to((me + step) % count).wait_send()
+
+    relay.receive_across(0)
+    relay.finish_sends(0)
     own_x.wait()
     own_w.wait()
 
@@ -241,16 +377,19 @@
     return pl.pallas_call(
         functools.partial(gather_kernel, count),
         out_shape=(
-            jax.ShapeDtypeStruct((count,) + stream.shape, jnp.bfloat16),
+            jax.ShapeDtypeStruct((1, count) + stream.shape, jnp.bfloat16),
             jax.ShapeDtypeStruct(heads, jnp.bfloat16),
         ),
-        in_specs=[vmem] * 3,
+        in_specs=[anywhere, vmem, anywhere],
         out_specs=(anywhere, anywhere),
         scratch_shapes=[
             pltpu.VMEM(stream.shape, jnp.bfloat16),
+            pltpu.VMEM(w_rows.shape, jnp.bfloat16),
+            pltpu.VMEM(stream.shape, jnp.bfloat16),
             pltpu.VMEM(heads, jnp.bfloat16),
-            sems((count,)), sems((count,)), sems((count,)), sems((count,)), sems((2,)),
-        ],
+        ]
+        + relay_sems(1, count)
+        + [sems((count,)), sems((count,)), sems((count,)), sems((4,))],
         compiler_params=pltpu.CompilerParams(
             collective_id=0, has_side_effects=True, vmem_limit_bytes=24 * 1024 * 1024
         ),
@@ -259,34 +398,38 @@
 
 
 def attend_kernel(
-    count, scale, length_ref, q_ref, k_ref, v_ref, rows_ref, out_ref, wall,
-    mixed_ref, landed, send_c, recv_c, send_w, recv_w, own_sem,
+    count, scale, length_ref, q_ref, k_ref, v_ref, out_any, pw1_any, out_ref, wall,
+    rows_ref, mixed_ref, landed, send_c, recv_c,
+    up, down, over, across, landed_w, twin_w, own_sem,
 ):
     me = lax.axis_index("tm")
     call = lax.axis_index("call")
-    y_peer = me + 2 - 4 * ((me // 2) % 2)
-    c_peer = me + 1 - 2 * (me % 2)
     twin = {"call": 1 - call, "tm": me}
+    relay = Relay(count, wall, (up, down, over, across, landed_w))
+    columns = rows_ref.shape[2]
+    sources = (
+        out_any,
+        pw1_any.at[:, pl.ds(0, columns)],
+        pw1_any.at[:, pl.ds(columns, columns)],
+    )
+    gets = [
+        pltpu.make_async_copy(source, rows_ref.at[part], own_sem.at[part])
+        for part, source in enumerate(sources)
+    ]
+    for get in gets:
+        get.start()
     greet([{"tm": (me + step) % count} for step in range(1, count)] + [twin])
-    sends = []
-
-    def push(source, part, owner, where):
-        copy = remote(
-            source, wall.at[part, owner], send_w.at[len(sends)], recv_w.at[part, owner], where
+    for get in gets:
+        get.wait()
+
+    def twin_copy(part, owner):
+        return remote(
+            wall.at[part, owner], wall.at[part, owner], twin_w.at[owner],
+            landed_w.at[part, owner], twin,
         )
-        copy.start()
-        sends.append(copy)
-
-    def arrived(part, owner):
-        remote(
-            wall.at[part, owner], wall.at[part, owner], send_w.at[0], recv_w.at[part, owner],
-            {"tm": c_peer},
-        ).wait_recv()
-
-    def relay(part, owner, places):
-        arrived(part, owner)
-        for where in places:
-            push(wall.at[part, owner], part, owner, where)
+
+    def to_twin(part, owner):
+        twin_copy(part, owner).start()
 
     width = LEFT + SPAN
     length = length_ref[call]
@@ -315,35 +458,31 @@
         ).start()
         return carry
 
-    hops = range(4, count, 4)
-    own = pltpu.make_async_copy(rows_ref, wall.at[:, me], own_sem.at[0])
+    own = pltpu.make_async_copy(rows_ref, wall.at[:, me], own_sem.at[3])
     own.start()
-    for hop in hops:
-        for part in (call, 2):
-            push(rows_ref.at[part], part, me, {"tm": (me + hop) % count})
     for part in (call, 2):
-        push(rows_ref.at[part], part, me, {"tm": y_peer})
+        relay.start(rows_ref.at[part], part)
     for part in range(3):
-        push(rows_ref.at[part], part, me, {"tm": c_peer})
+        relay.start_across(rows_ref.at[part], part)
+    steps = count // 4 - 1
+
+    def relay_step(at):
+        relay.step(at, call, to_twin)
+        relay.step(at, 2)
+        relay.step_over(at - 1, call, to_twin)
+        relay.step_over(at - 1, 2)
+
     lax.fori_loop(1, count // 2, attend_and_send, 0)
-    relay(call, y_peer, [twin, {"tm": c_peer}])
-    relay(2, y_peer, [{"tm": c_peer}])
-    relay(call, (me + 4) % count, [{"tm": y_peer}, twin, {"tm": c_peer}])
-    relay(2, (me + 4) % count, [{"tm": y_peer}, {"tm": c_peer}])
+    relay_step(0)
     lax.fori_loop(count // 2, count, attend_and_send, 0)
     landed[me] = attend(me)
-    for hop in range(8, count, 4):
-        owner = (me + hop) % count
-        relay(call, owner, [{"tm": y_peer}, twin, {"tm": c_peer}])
-        relay(2, owner, [{"tm": y_peer}, {"tm": c_peer}])
-    for hop in hops:
-        owner = (y_peer + hop) % count
-        relay(call, owner, [twin, {"tm": c_peer}])
-        relay(2, owner, [{"tm": c_peer}])
-    relay(1 - call, y_peer, [{"tm": c_peer}])
-    for hop in hops:
-        relay(1 - call, (me + hop) % count, [{"tm": c_peer}])
-        relay(1 - call, (y_peer + hop) % count, [{"tm": c_peer}])
+    for at in range(1, steps):
+        relay_step(at)
+    relay.step_over(steps - 1, call, to_twin)
+    relay.step_over(steps - 1, 2)
+    received = relay.column(me)[1:] + relay.column(relay.y_peer)
+    for owner in received:
+        relay.pass_across(1 - call, owner)
     for step in range(1, count):
         owner = (me + step) % count
         remote(
@@ -355,41 +494,44 @@
             [landed[pair], landed[pair + 1]], axis=1
         )
     own.wait()
-    both = c_peer + 2 - 4 * ((me // 2) % 2)
     for part in range(3):
-        for hop in range(0, count, 4):
-            arrived(part, (c_peer + hop) % count)
-            arrived(part, (both + hop) % count)
-    for copy in sends:
-        copy.wait_send()
-
-
-def attend_call(lengths, queries, keys, values, rows):
+        relay.receive_across(part)
+    for owner in received:
+        twin_copy(call, owner).wait_send()
+    relay.finish_sends(call)
+    relay.finish_sends(2)
+    for owner in relay.column(me) + relay.column(relay.y_peer):
+        relay.copy(wall.at[1 - call, owner], 1 - call, owner, across, relay.c_peer).wait_send()
+
+
+def attend_call(lengths, queries, keys, values, w_out, w_pw1):
     frames, width = queries.shape
     count = frames // SPAN
     anywhere = pl.BlockSpec(memory_space=pl.ANY)
     vmem = pl.BlockSpec(memory_space=pltpu.VMEM)
     sems = pltpu.SemaphoreType.DMA
-    parts, depth, columns = rows.shape
-    copies = 2 * (count // 4 - 1) + 5 + 3 + 5 * (count // 4 - 1) + 3 * (count // 4 - 1) + 7
+    parts, (depth, columns) = 3, w_out.shape
     return pl.pallas_call(
         functools.partial(attend_kernel, count, HEAD_DIM**-0.5),
         out_shape=(
             jax.ShapeDtypeStruct((SPAN, count * width), jnp.bfloat16),
             jax.ShapeDtypeStruct((parts, count, depth, columns), jnp.bfloat16),
         ),
-        in_specs=[pl.BlockSpec(memory_space=pltpu.SMEM), vmem, vmem, vmem, anywhere],
+        in_specs=[pl.BlockSpec(memory_space=pltpu.SMEM), vmem, vmem, vmem, anywhere, anywhere],
         out_specs=(vmem, anywhere),
         scratch_shapes=[
+            pltpu.VMEM((parts, depth, columns), jnp.bfloat16),
             pltpu.VMEM((count, SPAN, width), jnp.bfloat16),
             pltpu.VMEM((count, SPAN, width), jnp.bfloat16),
-            sems((count,)), sems((count,)), sems((copies,)), sems((parts, count)), sems((1,)),
-        ],
+            sems((count,)), sems((count,)),
+        ]
+        + relay_sems(parts, count)
+        + [sems((count,)), sems((4,))],
         compiler_params=pltpu.CompilerParams(
             collective_id=1, has_side_effects=True, vmem_limit_bytes=32 * 1024 * 1024
         ),
         name="attend_exchange",
-    )(lengths, queries, keys, values, rows)
+    )(lengths, queries, keys, values, w_out, w_pw1)
 
 
 def project_kernel(length_ref, context_ref, stream_ref, w_ref, gain_ref, attended_ref, gated_ref):
@@ -543,8 +685,7 @@
     queries = packed[:, :HEAD_DIM]
     keys = jnp.pad(packed[:, HEAD_DIM : 2 * HEAD_DIM], ((LEFT, 0), (0, 0)))
     values = jnp.pad(packed[:, 2 * HEAD_DIM :], ((LEFT, 0), (0, 0)))
-    rows = jnp.stack([w_out, w_pw1[:, :model_width], w_pw1[:, model_width:]])
-    context, weights = attend_call(lengths, queries, keys, values, rows)
+    context, weights = attend_call(lengths, queries, keys, values, w_out, w_pw1)
     weights = weights.reshape(3, model_width, model_width)
     attended, gated = project_call(lengths, context, stream, weights, ln_conv_gain[None])
     conv_act = conv_call(count, lengths, gated, dw_kernel, bn_gain[None], bn_bias[None])

time: 136 us -> 108 us (0.79)
  Pallas kernels: 128 us -> 102 us
    pallas_call x1, Pallas kernels: 26.1 us -> 16.1 us  [conv_call(): pl.pallas_call(functools.partial(conv_kernel, count), out_shape=jax.Shape...]
    pallas_call x1, Pallas kernels: 56.4 us -> 46.5 us  [attend_call(): pl.pallas_call(functools.partial(attend_kernel, count, HEAD_DIM ** (-0.5)...]
    pallas_call x1, Pallas kernels: 43.8 us -> 37.3 us  [gather_call(): pl.pallas_call(functools.partial(gather_kernel, count), out_shape=(jax.Sh...]
    unnamed x19 -> x23, local copies, waits for them, and re-layouts: 3.37 us -> 3.68 us
where the time goes in v3:
time: 108 us
  Pallas kernels  102 us (94%)
  local copies, waits for them, and re-layouts  4.27 us (4%)
  matrix products  1.28 us (1%)
    pallas_call x1, Pallas kernels, attend_call(): pl.pallas_call(functools.partial(attend_kernel, count, HEAD_DIM ** (-0.5)...  46.5 us
    pallas_call x1, Pallas kernels, gather_call(): pl.pallas_call(functools.partial(gather_kernel, count), out_shape=(jax.Sh...  37.3 us
    pallas_call x1, Pallas kernels, conv_call(): pl.pallas_call(functools.partial(conv_kernel, count), out_shape=jax.Shape...  16.1 us
    unnamed x23, local copies, waits for them, and re-layouts  3.68 us

profile of v3, /device:TPU:0, one launch (start us, length us, event | category | flops | bytes accessed | tf_op | source)
XLA Modules:
  0.0 108.1 jit_solution(8412774630975029397)
XLA Ops:
  0.6 0.0 copy-start
  0.6 0.9 copy-done
  1.6 0.0 copy-start.2
  1.6 1.0 copy-done.2
  2.6 0.0 copy-start.7
  2.6 0.7 copy-done.7
  3.3 37.3 %gather_frames.1 = (bf16[1,16,128,1024]{3,2,1,0:T(8,128)(2,1)S(1)}, bf16[16,64,192]{2,1,0:T(8,128)(2,1)S(1)}) custom-call(bf16[128,1024]{1,0:T(8,128)(2,1)S(1)} %bitcast.13, f32[1,1024]{1,0:T(1,128)S(1)} %bitcast.16, bf16[64,3072]{1,0:T(8,128)(2,1)S(1)} %copy-done.2), custom_call_target="tpu_custom_call" | custom-call | tf_op jit(solution)/shard_map/gather_frames/pallas_call | solution.py:377
  40.5 1.3 %convolution_convert_fusion = bf16[2048,192]{1,0:T(8,128)(2,1)S(1)} fusion(bf16[2048,1024]{1,0:T(8,128)(2,1)S(1)} %bitcast.20, bf16[1024,192]{1,0:T(8,128)(2,1)S(1)} %bitcast.21), kind=kOutput, calls=%fused_computation | convolution fusion | flops 805699584 | bytes 5373952 | tf_op jit(solution)/shard_map/dot_general | solution.py:47
  41.8 0.0 copy-start.3
  41.8 0.0 copy-start.4
  41.8 0.0 copy-start.6
  41.9 0.0 copy-start.1
  41.9 0.0 copy-start.8
  41.9 0.3 fusion
  42.2 0.1 pad.8.v_ref
  42.4 0.1 pad.7.k_ref
  42.5 0.3 copy-done.3
  42.8 0.0 copy-done.4
  42.8 0.0 copy-done.6
  42.8 0.0 copy-start.5
  42.8 0.0 copy-start.9
  42.8 0.0 copy-start.10
  42.8 46.5 %attend_exchange.1 = (bf16[128,1024]{1,0:T(8,128)(2,1)S(1)}, bf16[3,16,64,1024]{3,2,1,0:T(8,128)(2,1)S(1)}) custom-call(s32[2]{0:T(128)S(1)} %copy-done.6, bf16[2048,64]{1,0:T(8,128)(2,1)S(1)} %get-tuple-element.16.q_ref, bf16[3072,64]{1,0:T(8,128)(2,1)S(1)} %pad.7.k_ref, bf16[3072,64]{1,0:T(8,128)(2,1)S(1)} %pad.8.v_ref, bf16[64,1024]{1,0:T(8,128)(2,1)S(1)} %copy-done.4, ...), custom_call_target="tpu_custom_call" | custom-call | tf_op jit(solution)/shard_map/attend_exchange/pallas_call | solution.py:514
  89.3 0.0 copy-done.1
  89.3 0.0 copy-done.8
  89.3 1.9 %project_gate.1 = (bf16[128,1024]{1,0:T(8,128)(2,1)}, bf16[128,1024]{1,0:T(8,128)(2,1)S(1)}) custom-call(s32[2]{0:T(128)S(1)} %copy-done.6, bf16[128,1024]{1,0:T(8,128)(2,1)S(1)} %get-tuple-element.10.context_ref, bf16[128,1024]{1,0:T(8,128)(2,1)S(1)} %bitcast.14, bf16[3,1024,1024]{2,1,0:T(8,128)(2,1)S(1)} %bitcast.12, f32[1,1024]{1,0:T(1,128)S(1)} %bitcast.17), custom_call_target="tpu_custom_call" | custom-call | tf_op jit(solution)/shard_map/project_gate/pallas_call | solution.py:552
  91.3 0.0 copy-done.5
  91.3 0.0 copy-done.9
  91.3 0.0 copy-done.10
  91.3 16.1 %conv_norm.1 = bf16[128,1024]{1,0:T(8,128)(2,1)S(1)} custom-call(s32[2]{0:T(128)S(1)} %copy-done.6, bf16[128,1024]{1,0:T(8,128)(2,1)S(1)} %get-tuple-element.13.g_ref, f32[9,1024]{1,0:T(8,128)S(1)} %copy-done.5, f32[1,1024]{1,0:T(1,128)S(1)} %bitcast.18, f32[1,1024]{1,0:T(1,128)S(1)} %bitcast.19), custom_call_target="tpu_custom_call" | custom-call | tf_op jit(solution)/shard_map/conv_norm/pallas_call | solution.py:652
  107.4 0.7 copy.15
Async XLA Ops:
  0.6 1.0 copy-start
  1.6 1.0 copy-start.2
  2.6 0.7 copy-start.7
  41.8 1.0 copy-start.3
  41.8 1.0 copy-start.4
  41.8 1.0 copy-start.6
  41.9 47.5 %copy-start.1 = (bf16[1,128,1024]{2,1,0:T(8,128)(2,1)S(1)}, bf16[1,128,1024]{2,1,0:T(8,128)(2,1)}, u32[]{:S(2)}) copy-start(bf16[1,128,1024]{2,1,0:T(8,128)(2,1)} %param.10) | copy-start | bytes 786436
  41.9 47.5 %copy-start.8 = (f32[1024]{0:T(1024)S(1)}, f32[1024]{0:T(1024)}, u32[]{:S(2)}) copy-start(f32[1024]{0:T(1024)} %param.15) | copy-start | bytes 12292
  42.8 48.5 %copy-start.5 = (f32[9,1024]{1,0:T(8,128)S(1)}, f32[9,1024]{1,0:T(8,128)}, u32[]{:S(2)}) copy-start(f32[9,1024]{1,0:T(8,128)} %taps_ref.1) | copy-start | bytes 110596
  42.8 48.5 %copy-start.9 = (f32[1024]{0:T(1024)S(1)}, f32[1024]{0:T(1024)}, u32[]{:S(2)}) copy-start(f32[1024]{0:T(1024)} %param.18) | copy-start | bytes 12292
  42.8 48.5 %copy-start.10 = (f32[1024]{0:T(1024)S(1)}, f32[1024]{0:T(1024)}, u32[]{:S(2)}) copy-start(f32[1024]{0:T(1024)} %param.19) | copy-start | bytes 12292

commit v4 on v3

--- a/solution.py
+++ b/solution.py
@@ -149,11 +149,8 @@
     )
 
 
-def greet(places):
-    barrier = pltpu.get_barrier_semaphore()
-    for where in places:
-        pl.semaphore_signal(barrier, inc=1, device_id=where, device_id_type=MESH)
-    pl.semaphore_wait(barrier, len(places))
+EDGE = 16
+STRIP = 128
 
 
 class Relay:
@@ -283,25 +280,61 @@
     return [pltpu.SemaphoreType.DMA((parts, count)) for _ in range(5)]
 
 
-def gather_kernel(
-    count, stream_any, gain_ref, rows_any, xall, wcol, stream_ref, rows_ref, x_ref, w_ref,
-    up, down, over, across, landed, send_w, recv_w, twin_w, own_sem,
+def layer_kernel(
+    count, scale, length_ref, stream_any, gain1_any, rows_any, out_any, gain2_any, pw1_any,
+    taps_any, bn_gain_any, bn_bias_any, attended_ref, out_ref,
+    stream_ref, gain1_ref, rows_ref, gain2_ref, taps_ref, gain_ref, bias_ref,
+    x_ref, w_ref, xall, wcol, q_ref, k_ref, v_ref, parts_ref, wall, mixed_ref, landed,
+    context, g_ref, low, high, padded, depth, mine, plane, near, far,
+    f_up, f_down, f_over, f_across, f_landed, send_w, recv_w, twin_f,
+    up, down, over, across, landed_w, twin_w, send_c, recv_c,
+    halo_send, halo_recv, near_send, near_recv, far_send, far_recv, own_sem, get_sem,
 ):
     me = lax.axis_index("tm")
     call = lax.axis_index("call")
     twin = {"call": 1 - call, "tm": me}
-    relay = Relay(count, xall, (up, down, over, across, landed))
-    get_stream = pltpu.make_async_copy(stream_any, stream_ref, own_sem.at[0])
-    get_rows = pltpu.make_async_copy(rows_any, rows_ref, own_sem.at[1])
-    get_stream.start()
-    get_rows.start()
+    frames = Relay(count, xall, (f_up, f_down, f_over, f_across, f_landed))
+    relay = Relay(count, wall, (up, down, over, across, landed_w))
+    columns = parts_ref.shape[2]
+    loads = (
+        (stream_any, stream_ref),
+        (gain1_any, gain1_ref),
+        (rows_any, rows_ref),
+        (out_any, parts_ref.at[0]),
+        (pw1_any.at[:, pl.ds(0, columns)], parts_ref.at[1]),
+        (pw1_any.at[:, pl.ds(columns, columns)], parts_ref.at[2]),
+        (gain2_any, gain2_ref),
+        (taps_any, taps_ref),
+        (bn_gain_any, gain_ref),
+        (bn_bias_any, bias_ref),
+    )
+    gets = [
+        pltpu.make_async_copy(source, target, get_sem.at[at])
+        for at, (source, target) in enumerate(loads)
+    ]
+    for get in gets:
+        get.start()
+    peers = []
+    for flips in range(1, 8):
+        spot, side = me, call
+        if flips & 1:
+            spot = spot + 1 - 2 * (me % 2)
+        if flips & 2:
+            spot = spot + 2 - 4 * ((me // 2) % 2)
+        if flips & 4:
+            side = 1 - call
+        peers.append({"call": side, "tm": spot})
+    hops = [{"tm": (me + hop) % count} for hop in range(4, count, 4)]
     barrier = pltpu.get_barrier_semaphore()
-    places = [{"tm": (me + step) % count} for step in range(1, count)] + [twin]
+    places = [{"tm": (me + step) % count} for step in range(1, count)]
+    places = places + [where for at, where in enumerate(peers) if at >= 3]
     for where in places:
         pl.semaphore_signal(barrier, inc=1, device_id=where, device_id_type=MESH)
-    get_stream.wait()
-    x_ref[...] = layer_norm(stream_ref[...], gain_ref[...]).astype(jnp.bfloat16)
-    get_rows.wait()
+    k_ref[0:LEFT, :] = jnp.zeros((LEFT, HEAD_DIM), jnp.bfloat16)
+    v_ref[0:LEFT, :] = jnp.zeros((LEFT, HEAD_DIM), jnp.bfloat16)
+    for get in gets:
+        get.wait()
+    x_ref[...] = layer_norm(stream_ref[...], gain1_ref[...]).astype(jnp.bfloat16)
     width = rows_ref.shape[1] // 3
     for head in range(count):
         for part in range(3):
@@ -309,12 +342,12 @@
             w_ref[head, :, part * HEAD_DIM : (part + 1) * HEAD_DIM] = rows_ref[
                 :, start : start + HEAD_DIM
             ]
-    own_x = pltpu.make_async_copy(x_ref, xall.at[0, me], own_sem.at[2])
-    own_w = pltpu.make_async_copy(w_ref.at[me], wcol.at[me], own_sem.at[3])
+    own_x = pltpu.make_async_copy(x_ref, xall.at[0, me], own_sem.at[0])
+    own_w = pltpu.make_async_copy(w_ref.at[me], wcol.at[me], own_sem.at[1])
     own_x.start()
     own_w.start()
     pl.semaphore_wait(barrier, len(places))
-    relay.start(x_ref, 0)
+    frames.start(x_ref, 0)
 
     def slice_to(place):
         return remote(
@@ -322,17 +355,17 @@
         )
 
     def slice_on(owner):
-        return remote(wcol.at[owner], wcol.at[owner], twin_w.at[owner], recv_w.at[owner], twin)
+        return remote(wcol.at[owner], wcol.at[owner], twin_f.at[owner], recv_w.at[owner], twin)
 
     @pl.when(me % 2 == call)
     def _():
         for step in range(1, count):
             slice_to((me + step) % count).start()
 
-    relay.start_across(x_ref, 0)
+    frames.start_across(x_ref, 0)
     steps = count // 4 - 1
-    relay.step(0, 0)
-    relay.step_over(-1, 0)
+    frames.step(0, 0)
+    frames.step_over(-1, 0)
     for pair in range(count // 2):
         owner = 2 * pair + call
 
@@ -342,9 +375,15 @@
             slice_on(owner).start()
 
     for at in range(1, steps):
-        relay.step(at, 0)
-        relay.step_over(at - 1, 0)
-    relay.step_over(steps - 1, 0)
+        frames.step(at, 0)
+        frames.step_over(at - 1, 0)
+    frames.step_over(steps - 1, 0)
+    own = pltpu.make_async_copy(parts_ref, wall.at[:, me], own_sem.at[2])
+    own.start()
+    for part in (call, 2):
+        relay.start(parts_ref.at[part], part)
+    for part in range(3):
+        relay.start_across(parts_ref.at[part], part)
     for pair in range(count // 2):
         owner, other = 2 * pair + call, 2 * pair + 1 - call
 
@@ -361,66 +400,20 @@
         for step in range(1, count):
             slice_to((me + step) % count).wait_send()
 
-    relay.receive_across(0)
-    relay.finish_sends(0)
     own_x.wait()
     own_w.wait()
-
-
-def gather_call(stream, gain, w_rows):
-    count = lax.axis_size("tm")
-    depth = w_rows.shape[0]
-    heads = (count, depth, 3 * HEAD_DIM)
-    anywhere = pl.BlockSpec(memory_space=pl.ANY)
-    vmem = pl.BlockSpec(memory_space=pltpu.VMEM)
-    sems = pltpu.SemaphoreType.DMA
-    return pl.pallas_call(
-        functools.partial(gather_kernel, count),
-        out_shape=(
-            jax.ShapeDtypeStruct((1, count) + stream.shape, jnp.bfloat16),
-            jax.ShapeDtypeStruct(heads, jnp.bfloat16),
-        ),
-        in_specs=[anywhere, vmem, anywhere],
-        out_specs=(anywhere, anywhere),
-        scratch_shapes=[
-            pltpu.VMEM(stream.shape, jnp.bfloat16),
-            pltpu.VMEM(w_rows.shape, jnp.bfloat16),
-            pltpu.VMEM(stream.shape, jnp.bfloat16),
-            pltpu.VMEM(heads, jnp.bfloat16),
-        ]
-        + relay_sems(1, count)
-        + [sems((count,)), sems((count,)), sems((count,)), sems((4,))],
-        compiler_params=pltpu.CompilerParams(
-            collective_id=0, has_side_effects=True, vmem_limit_bytes=24 * 1024 * 1024
-        ),
-        name="gather_frames",
-    )(stream, gain, w_rows)
-
-
-def attend_kernel(
-    count, scale, length_ref, q_ref, k_ref, v_ref, out_any, pw1_any, out_ref, wall,
-    rows_ref, mixed_ref, landed, send_c, recv_c,
-    up, down, over, across, landed_w, twin_w, own_sem,
-):
-    me = lax.axis_index("tm")
-    call = lax.axis_index("call")
-    twin = {"call": 1 - call, "tm": me}
-    relay = Relay(count, wall, (up, down, over, across, landed_w))
-    columns = rows_ref.shape[2]
-    sources = (
-        out_any,
-        pw1_any.at[:, pl.ds(0, columns)],
-        pw1_any.at[:, pl.ds(columns, columns)],
-    )
-    gets = [
-        pltpu.make_async_copy(source, rows_ref.at[part], own_sem.at[part])
-        for part, source in enumerate(sources)
-    ]
-    for get in gets:
-        get.start()
-    greet([{"tm": (me + step) % count} for step in range(1, count)] + [twin])
-    for get in gets:
-        get.wait()
+    frames.receive_across(0)
+    w_columns = wcol[...].reshape(-1, 3 * HEAD_DIM)
+
+    def project_block(block, carry):
+        first = pl.multiple_of(block * SPAN, SPAN)
+        packed = contract_with(xall[0, block], w_columns).astype(jnp.bfloat16)
+        q_ref[pl.ds(first, SPAN), :] = packed[:, :HEAD_DIM]
+        k_ref[pl.ds(first + LEFT, SPAN), :] = packed[:, HEAD_DIM : 2 * HEAD_DIM]
+        v_ref[pl.ds(first + LEFT, SPAN), :] = packed[:, 2 * HEAD_DIM :]
+        return carry
+
+    lax.fori_loop(0, count, project_block, 0)
 
     def twin_copy(part, owner):
         return remote(
@@ -457,14 +450,6 @@
             mixed_ref.at[place], landed.at[me], send_c.at[place], recv_c.at[me], {"tm": place}
         ).start()
         return carry
-
-    own = pltpu.make_async_copy(rows_ref, wall.at[:, me], own_sem.at[3])
-    own.start()
-    for part in (call, 2):
-        relay.start(rows_ref.at[part], part)
-    for part in range(3):
-        relay.start_across(rows_ref.at[part], part)
-    steps = count // 4 - 1
 
     def relay_step(at):
         relay.step(at, call, to_twin)
@@ -490,100 +475,23 @@
             {"tm": owner},
         ).wait()
     for pair in range(0, count, 2):
-        out_ref[:, pair * HEAD_DIM : (pair + 2) * HEAD_DIM] = jnp.concatenate(
+        context[:, pair * HEAD_DIM : (pair + 2) * HEAD_DIM] = jnp.concatenate(
             [landed[pair], landed[pair + 1]], axis=1
         )
     own.wait()
     for part in range(3):
         relay.receive_across(part)
-    for owner in received:
-        twin_copy(call, owner).wait_send()
-    relay.finish_sends(call)
-    relay.finish_sends(2)
-    for owner in relay.column(me) + relay.column(relay.y_peer):
-        relay.copy(wall.at[1 - call, owner], 1 - call, owner, across, relay.c_peer).wait_send()
-
-
-def attend_call(lengths, queries, keys, values, w_out, w_pw1):
-    frames, width = queries.shape
-    count = frames // SPAN
-    anywhere = pl.BlockSpec(memory_space=pl.ANY)
-    vmem = pl.BlockSpec(memory_space=pltpu.VMEM)
-    sems = pltpu.SemaphoreType.DMA
-    parts, (depth, columns) = 3, w_out.shape
-    return pl.pallas_call(
-        functools.partial(attend_kernel, count, HEAD_DIM**-0.5),
-        out_shape=(
-            jax.ShapeDtypeStruct((SPAN, count * width), jnp.bfloat16),
-            jax.ShapeDtypeStruct((parts, count, depth, columns), jnp.bfloat16),
-        ),
-        in_specs=[pl.BlockSpec(memory_space=pltpu.SMEM), vmem, vmem, vmem, anywhere, anywhere],
-        out_specs=(vmem, anywhere),
-        scratch_shapes=[
-            pltpu.VMEM((parts, depth, columns), jnp.bfloat16),
-            pltpu.VMEM((count, SPAN, width), jnp.bfloat16),
-            pltpu.VMEM((count, SPAN, width), jnp.bfloat16),
-            sems((count,)), sems((count,)),
-        ]
-        + relay_sems(parts, count)
-        + [sems((count,)), sems((4,))],
-        compiler_params=pltpu.CompilerParams(
-            collective_id=1, has_side_effects=True, vmem_limit_bytes=32 * 1024 * 1024
-        ),
-        name="attend_exchange",
-    )(lengths, queries, keys, values, w_out, w_pw1)
-
-
-def project_kernel(length_ref, context_ref, stream_ref, w_ref, gain_ref, attended_ref, gated_ref):
-    rows = stream_ref.shape[0]
-    first = lax.axis_index("tm") * rows
-    length = length_ref[lax.axis_index("call")]
-    valid = first + lax.broadcasted_iota(jnp.int32, (rows, 1), 0) < length
-    wide = stream_ref[...].astype(jnp.float32) + contract_with(context_ref[...], w_ref[0])
+    rows, width = depth.shape
+    valid = me * rows + lax.broadcasted_iota(jnp.int32, (rows, 1), 0) < length
+    weights = [wall[part].reshape(width, width) for part in range(3)]
+    wide = stream_ref[...].astype(jnp.float32) + contract_with(context[...], weights[0])
     attended = jnp.where(valid, wide, 0.0).astype(jnp.bfloat16)
     attended_ref[...] = attended
-    conv_in = layer_norm(attended, gain_ref[...]).astype(jnp.bfloat16)
-    gated = contract_with(conv_in, w_ref[1]) * jax.nn.sigmoid(contract_with(conv_in, w_ref[2]))
-    gated_ref[...] = jnp.where(valid, gated, 0.0).astype(jnp.bfloat16)
-
-
-def project_call(lengths, context, stream, weights, gain):
-    vmem = pl.BlockSpec(memory_space=pltpu.VMEM)
-    return pl.pallas_call(
-        project_kernel,
-        out_shape=(jax.ShapeDtypeStruct(stream.shape, jnp.bfloat16),) * 2,
-        in_specs=[pl.BlockSpec(memory_space=pltpu.SMEM)] + [vmem] * 4,
-        out_specs=(vmem, vmem),
-        compiler_params=pltpu.CompilerParams(vmem_limit_bytes=32 * 1024 * 1024),
-        name="project_gate",
-    )(lengths, context, stream, weights, gain)
-
-
-EDGE = 16
-STRIP = 128
-
-
-def conv_kernel(
-    count, length_ref, g_ref, taps_ref, gain_ref, bias_ref, out_ref,
-    low, high, padded, depth, mine, plane, near, far,
-    halo_send, halo_recv, near_send, near_recv, far_send, far_recv,
-):
-    me = lax.axis_index("tm")
-    call = lax.axis_index("call")
-    rows, width = depth.shape
+    conv_in = layer_norm(attended, gain2_ref[...]).astype(jnp.bfloat16)
+    gate = jax.nn.sigmoid(contract_with(conv_in, weights[2]))
+    gated = contract_with(conv_in, weights[1]) * gate
+    g_ref[...] = jnp.where(valid, gated, 0.0).astype(jnp.bfloat16)
     right, left = (me + 1) % count, (me + count - 1) % count
-    peers = []
-    for flips in range(1, 8):
-        spot, side = me, call
-        if flips & 1:
-            spot = spot + 1 - 2 * (me % 2)
-        if flips & 2:
-            spot = spot + 2 - 4 * ((me // 2) % 2)
-        if flips & 4:
-            side = 1 - call
-        peers.append({"call": side, "tm": spot})
-    hops = [{"tm": (me + hop) % count} for hop in range(4, count, 4)]
-    greet([{"tm": right}, {"tm": left}] + peers + hops)
     to_right = remote(
         g_ref.at[pl.ds(rows - EDGE, EDGE)], low, halo_send.at[0], halo_recv.at[0], {"tm": right}
     )
@@ -644,51 +552,63 @@
         copy.wait_send()
 
 
-def conv_call(count, lengths, gated, taps, gain, bias):
-    rows, width = gated.shape
+    for owner in received:
+        twin_copy(call, owner).wait_send()
+    relay.finish_sends(call)
+    relay.finish_sends(2)
+    for owner in relay.column(me) + relay.column(relay.y_peer):
+        relay.copy(wall.at[1 - call, owner], 1 - call, owner, across, relay.c_peer).wait_send()
+    frames.finish_sends(0)
+
+
+def layer_call(lengths, stream, gain1, w_qkv, w_out, gain2, w_pw1, taps, bn_gain, bn_bias):
+    rows, width = stream.shape
+    count = lax.axis_size("tm")
+    wide, deep = jnp.float32, jnp.bfloat16
+    depth, planes = w_out.shape[0], count // 4
+    total = count * rows
+    anywhere = pl.BlockSpec(memory_space=pl.ANY)
     vmem = pl.BlockSpec(memory_space=pltpu.VMEM)
+    buffers = [
+        (stream.shape, deep), ((1, width), wide), (w_qkv.shape, deep), ((1, width), wide),
+        (taps.shape, wide), ((1, width), wide), ((1, width), wide),
+        (stream.shape, deep), ((count, depth, 3 * HEAD_DIM), deep),
+        ((1, count, rows, width), deep), ((count, depth, 3 * HEAD_DIM), deep),
+        ((total, HEAD_DIM), deep), ((total + LEFT, HEAD_DIM), deep),
+        ((total + LEFT, HEAD_DIM), deep),
+        ((3, depth, width), deep), ((3, count, depth, width), deep),
+        ((count, rows, HEAD_DIM), deep), ((count, rows, HEAD_DIM), deep),
+        (stream.shape, deep), (stream.shape, deep), ((EDGE, width), deep), ((EDGE, width), deep),
+        ((rows + 2 * EDGE, width), wide), ((rows, width), wide), ((2, width), wide),
+        ((2, width), wide), ((7, 2, width), wide), ((planes - 1, 2, width), wide),
+    ]
+    counts = [(count,)] * 3, [(count,)] * 3, [2, 2, 7, 7, planes - 1, planes - 1, 3, 10]
     sems = pltpu.SemaphoreType.DMA
-    far_count = count // 4 - 1
     return pl.pallas_call(
-        functools.partial(conv_kernel, count),
-        out_shape=jax.ShapeDtypeStruct(gated.shape, jnp.bfloat16),
-        in_specs=[pl.BlockSpec(memory_space=pltpu.SMEM)] + [vmem] * 4,
-        out_specs=vmem,
-        scratch_shapes=[
-            pltpu.VMEM((EDGE, width), jnp.bfloat16),
-            pltpu.VMEM((EDGE, width), jnp.bfloat16),
-            pltpu.VMEM((rows + 2 * EDGE, width), jnp.float32),
-            pltpu.VMEM((rows, width), jnp.float32),
-            pltpu.VMEM((2, width), jnp.float32),
-            pltpu.VMEM((2, width), jnp.float32),
-            pltpu.VMEM((7, 2, width), jnp.float32),
-            pltpu.VMEM((far_count, 2, width), jnp.float32),
-            sems((2,)), sems((2,)), sems((7,)), sems((7,)), sems((far_count,)), sems((far_count,)),
-        ],
+        functools.partial(layer_kernel, count, HEAD_DIM**-0.5),
+        out_shape=(jax.ShapeDtypeStruct(stream.shape, deep),) * 2,
+        in_specs=[pl.BlockSpec(memory_space=pltpu.SMEM)] + [anywhere] * 9,
+        out_specs=(vmem, vmem),
+        scratch_shapes=[pltpu.VMEM(shape, kind) for shape, kind in buffers]
+        + relay_sems(1, count)
+        + [sems(shape) for shape in counts[0]]
+        + relay_sems(3, count)
+        + [sems(shape) for shape in counts[1]]
+        + [sems((size,)) for size in counts[2]],
         compiler_params=pltpu.CompilerParams(
-            collective_id=2, has_side_effects=True, vmem_limit_bytes=32 * 1024 * 1024
+            collective_id=0, has_side_effects=True, vmem_limit_bytes=48 * 1024 * 1024
         ),
-        name="conv_norm",
-    )(lengths, gated, taps, gain, bias)
+        name="layer",
+    )(lengths, stream, gain1, w_qkv, w_out, gain2, w_pw1, taps, bn_gain, bn_bias)
 
 
 def one_head_each(
     frames, lengths, ln_attn_gain, w_qkv, w_out, ln_conv_gain, w_pw1, dw_kernel, bn_gain, bn_bias
 ):
-    stream = frames[0]
-    model_width = stream.shape[1]
-    count = lax.axis_size("tm")
-    all_frames, w_columns = gather_call(stream, ln_attn_gain[None], w_qkv)
-    packed = contract_with(
-        all_frames.reshape(-1, model_width), w_columns.reshape(model_width, -1)
-    ).astype(jnp.bfloat16)
-    queries = packed[:, :HEAD_DIM]
-    keys = jnp.pad(packed[:, HEAD_DIM : 2 * HEAD_DIM], ((LEFT, 0), (0, 0)))
-    values = jnp.pad(packed[:, 2 * HEAD_DIM :], ((LEFT, 0), (0, 0)))
-    context, weights = attend_call(lengths, queries, keys, values, w_out, w_pw1)
-    weights = weights.reshape(3, model_width, model_width)
-    attended, gated = project_call(lengths, context, stream, weights, ln_conv_gain[None])
-    conv_act = conv_call(count, lengths, gated, dw_kernel, bn_gain[None], bn_bias[None])
+    attended, conv_act = layer_call(
+        lengths, frames[0], ln_attn_gain[None], w_qkv, w_out, ln_conv_gain[None], w_pw1,
+        dw_kernel, bn_gain[None], bn_bias[None],
+    )
     return (attended[None], conv_act[None])
 
 

time: 108 us -> 101 us (0.935)
  Pallas kernels: 102 us -> 91.7 us
  local copies, waits for them, and re-layouts: 4.27 us -> 8.1 us
  matrix products: 1.28 us -> 0 us
    pallas_call x4 -> x1, Pallas kernels: 102 us -> 91.7 us  [layer_call(): pl.pallas_call(functools.partial(layer_kernel, count, HEAD_DIM ** (-0.5))...]
    unnamed x23 -> x22, local copies, waits for them, and re-layouts: 3.68 us -> 8.1 us
    dot_general x1 -> x0, matrix products: 1.28 us -> none  [contract_with(): return jnp.dot(left, rows_piece, preferred_element_type=jnp.float32)]
where the time goes in v4:
time: 101 us; the launch traced here: 100 us
  Pallas kernels  91.7 us (91%)
  local copies, waits for them, and re-layouts  8.1 us (8%)
    pallas_call x1, Pallas kernels, layer_call(): pl.pallas_call(functools.partial(layer_kernel, count, HEAD_DIM ** (-0.5))...  91.7 us
    unnamed x22, local copies, waits for them, and re-layouts  8.1 us

profile of v4, /device:TPU:0, one launch (start us, length us, event | category | flops | bytes accessed | tf_op | source)
XLA Modules:
  0.0 100.4 jit_solution(16293526055161526304)
XLA Ops:
  0.6 0.0 copy-start.6
  0.6 0.0 copy-start.5
  0.7 0.0 copy-start.9
  0.7 0.7 copy-done.6
  1.3 0.0 copy-done.5
  1.3 0.0 copy-done.9
  1.3 0.0 copy-start
  1.3 1.0 copy-done
  2.3 0.0 copy-start.1
  2.3 0.9 copy-done.1
  3.3 0.0 copy-start.2
  3.3 0.9 copy-done.2
  4.2 0.0 copy-start.3
  4.2 0.9 copy-done.3
  5.1 0.0 copy-start.4
  5.1 0.8 copy-done.4
  6.0 0.0 copy-start.7
  6.0 0.7 copy-done.7
  6.7 0.0 copy-start.8
  6.7 0.7 copy-done.8
  7.4 91.7 %layer.1 = (bf16[128,1024]{1,0:T(8,128)(2,1)S(1)}, bf16[128,1024]{1,0:T(8,128)(2,1)S(1)}) custom-call(s32[2]{0:T(128)S(1)} %copy-done.9, bf16[128,1024]{1,0:T(8,128)(2,1)S(1)} %bitcast.9, f32[1,1024]{1,0:T(1,128)S(1)} %bitcast.10, bf16[64,3072]{1,0:T(8,128)(2,1)S(1)} %copy-done, bf16[64,1024]{1,0:T(8,128)(2,1)S(1)} %copy-done.3, f32[1,1024]{1,0:T(1,128)S(1)} %bitcast.11, ...), custom_call_target="tpu_custom_call" | custom-call | tf_op jit(solution)/shard_map/layer/pallas_call | solution.py:587
  99.0 0.7 copy.14
  99.7 0.7 copy.15
Async XLA Ops:
  0.6 0.7 copy-start.6
  0.6 0.7 copy-start.5
  0.7 0.7 copy-start.9
  1.3 1.0 copy-start
  2.3 0.9 copy-start.1
  3.3 0.9 copy-start.2
  4.2 0.9 copy-start.3
  5.1 0.8 copy-start.4
  6.0 0.7 copy-start.7
  6.7 0.7 copy-start.8

commit v5 on v4

--- a/solution.py
+++ b/solution.py
@@ -154,9 +154,9 @@
 
 
 class Relay:
-    def __init__(self, count, buffer, sems):
+    def __init__(self, count, slot, sems):
         self.count = count
-        self.buffer = buffer
+        self.held = slot
         self.up, self.down, self.over, self.across, self.landed = sems
         self.me = lax.axis_index("tm")
         self.planes = count // 4
@@ -167,14 +167,11 @@
     def copy(self, source, part, owner, send, place):
         return remote(
             source,
-            self.buffer.at[part, owner],
+            self.held(part, owner),
             send.at[part, owner],
             self.landed.at[part, owner],
             {"tm": place % self.count},
         )
-
-    def held(self, part, owner):
-        return self.buffer.at[part, owner]
 
     def arrived(self, part, owner):
         self.copy(self.held(part, owner), part, owner, self.across, self.c_peer).wait_recv()
@@ -293,16 +290,23 @@
     me = lax.axis_index("tm")
     call = lax.axis_index("call")
     twin = {"call": 1 - call, "tm": me}
-    frames = Relay(count, xall, (f_up, f_down, f_over, f_across, f_landed))
-    relay = Relay(count, wall, (up, down, over, across, landed_w))
-    columns = parts_ref.shape[2]
+    frames = Relay(count, lambda part, owner: xall.at[part, owner], (f_up, f_down, f_over, f_across, f_landed))
+    columns = stream_ref.shape[1]
+    half = parts_ref.shape[0] // 2
+
+    def half_of(part):
+        return pl.ds(pl.multiple_of(part * half, half), half)
+
+    def weight_slot(part, owner):
+        return wall.at[owner, half_of(part)]
+
+    relay = Relay(count, weight_slot, (up, down, over, across, landed_w))
     loads = (
         (stream_any, stream_ref),
         (gain1_any, gain1_ref),
         (rows_any, rows_ref),
-        (out_any, parts_ref.at[0]),
-        (pw1_any.at[:, pl.ds(0, columns)], parts_ref.at[1]),
-        (pw1_any.at[:, pl.ds(columns, columns)], parts_ref.at[2]),
+        (out_any, parts_ref.at[:, pl.ds(0, columns)]),
+        (pw1_any, parts_ref.at[:, pl.ds(columns, 2 * columns)]),
         (gain2_any, gain2_ref),
         (taps_any, taps_ref),
         (bn_gain_any, gain_ref),
@@ -332,9 +336,17 @@
         pl.semaphore_signal(barrier, inc=1, device_id=where, device_id_type=MESH)
     k_ref[0:LEFT, :] = jnp.zeros((LEFT, HEAD_DIM), jnp.bfloat16)
     v_ref[0:LEFT, :] = jnp.zeros((LEFT, HEAD_DIM), jnp.bfloat16)
-    for get in gets:
+    gets[0].wait()
+    gets[1].wait()
+    x_ref[...] = layer_norm(stream_ref[...], gain1_ref[...]).astype(jnp.bfloat16)
+    own_x = pltpu.make_async_copy(x_ref, xall.at[0, me], own_sem.at[0])
+    own_w = pltpu.make_async_copy(w_ref.at[me], wcol.at[me], own_sem.at[1])
+    own_x.start()
+    pl.semaphore_wait(barrier, len(places))
+    frames.start(x_ref, 0)
+    frames.start_across(x_ref, 0)
+    for get in gets[2:]:
         get.wait()
-    x_ref[...] = layer_norm(stream_ref[...], gain1_ref[...]).astype(jnp.bfloat16)
     width = rows_ref.shape[1] // 3
     for head in range(count):
         for part in range(3):
@@ -342,12 +354,7 @@
             w_ref[head, :, part * HEAD_DIM : (part + 1) * HEAD_DIM] = rows_ref[
                 :, start : start + HEAD_DIM
             ]
-    own_x = pltpu.make_async_copy(x_ref, xall.at[0, me], own_sem.at[0])
-    own_w = pltpu.make_async_copy(w_ref.at[me], wcol.at[me], own_sem.at[1])
-    own_x.start()
     own_w.start()
-    pl.semaphore_wait(barrier, len(places))
-    frames.start(x_ref, 0)
 
     def slice_to(place):
         return remote(
@@ -362,7 +369,6 @@
         for step in range(1, count):
             slice_to((me + step) % count).start()
 
-    frames.start_across(x_ref, 0)
     steps = count // 4 - 1
     frames.step(0, 0)
     frames.step_over(-1, 0)
@@ -378,12 +384,11 @@
         frames.step(at, 0)
         frames.step_over(at - 1, 0)
     frames.step_over(steps - 1, 0)
-    own = pltpu.make_async_copy(parts_ref, wall.at[:, me], own_sem.at[2])
+    own = pltpu.make_async_copy(parts_ref, wall.at[me], own_sem.at[2])
     own.start()
-    for part in (call, 2):
-        relay.start(parts_ref.at[part], part)
-    for part in range(3):
-        relay.start_across(parts_ref.at[part], part)
+    relay.start(parts_ref.at[half_of(call)], call)
+    for part in range(2):
+        relay.start_across(parts_ref.at[half_of(part)], part)
     for pair in range(count // 2):
         owner, other = 2 * pair + call, 2 * pair + 1 - call
 
@@ -405,20 +410,22 @@
     frames.receive_across(0)
     w_columns = wcol[...].reshape(-1, 3 * HEAD_DIM)
 
-    def project_block(block, carry):
-        first = pl.multiple_of(block * SPAN, SPAN)
-        packed = contract_with(xall[0, block], w_columns).astype(jnp.bfloat16)
-        q_ref[pl.ds(first, SPAN), :] = packed[:, :HEAD_DIM]
-        k_ref[pl.ds(first + LEFT, SPAN), :] = packed[:, HEAD_DIM : 2 * HEAD_DIM]
-        v_ref[pl.ds(first + LEFT, SPAN), :] = packed[:, 2 * HEAD_DIM :]
+    group = 4 * SPAN
+
+    def project_group(at, carry):
+        first = pl.multiple_of(at * group, group)
+        rows = xall[0, pl.ds(4 * at, 4)].reshape(group, columns)
+        packed = contract_with(rows, w_columns).astype(jnp.bfloat16)
+        q_ref[pl.ds(first, group), :] = packed[:, :HEAD_DIM]
+        k_ref[pl.ds(first + LEFT, group), :] = packed[:, HEAD_DIM : 2 * HEAD_DIM]
+        v_ref[pl.ds(first + LEFT, group), :] = packed[:, 2 * HEAD_DIM :]
         return carry
 
-    lax.fori_loop(0, count, project_block, 0)
+    lax.fori_loop(0, count // 4, project_group, 0)
 
     def twin_copy(part, owner):
         return remote(
-            wall.at[part, owner], wall.at[part, owner], twin_w.at[owner],
-            landed_w.at[part, owner], twin,
+            weight_slot(part, owner), weight_slot(part, owner), twin_w.at[owner], landed_w.at[part, owner], twin
         )
 
     def to_twin(part, owner):
@@ -439,7 +446,9 @@
         query_pos = block * SPAN + lax.broadcasted_iota(jnp.int32, (SPAN, width), 0)
         allowed = (key_pos >= 0) & ((key_pos < length) | (key_pos == query_pos))
         raised = jnp.where(allowed, jnp.exp(scores * scale), 0.0)
-        probs = (raised / jnp.sum(raised, axis=-1, keepdims=True)).astype(jnp.bfloat16)
+        total = jnp.sum(raised, axis=-1, keepdims=True)
+        shrink = jnp.where(total > 1.0, 2.0**-32, 1.0).astype(jnp.float32)
+        probs = (raised * shrink * (1.0 / (total * shrink))).astype(jnp.bfloat16)
         mixed = jnp.dot(probs, v_ref[pl.ds(first, width), :], preferred_element_type=jnp.float32)
         return mixed.astype(jnp.bfloat16)
 
@@ -453,9 +462,7 @@
 
     def relay_step(at):
         relay.step(at, call, to_twin)
-        relay.step(at, 2)
         relay.step_over(at - 1, call, to_twin)
-        relay.step_over(at - 1, 2)
 
     lax.fori_loop(1, count // 2, attend_and_send, 0)
     relay_step(0)
@@ -464,7 +471,6 @@
     for at in range(1, steps):
         relay_step(at)
     relay.step_over(steps - 1, call, to_twin)
-    relay.step_over(steps - 1, 2)
     received = relay.column(me)[1:] + relay.column(relay.y_peer)
     for owner in received:
         relay.pass_across(1 - call, owner)
@@ -479,11 +485,13 @@
             [landed[pair], landed[pair + 1]], axis=1
         )
     own.wait()
-    for part in range(3):
+    for part in range(2):
         relay.receive_across(part)
     rows, width = depth.shape
     valid = me * rows + lax.broadcasted_iota(jnp.int32, (rows, 1), 0) < length
-    weights = [wall[part].reshape(width, width) for part in range(3)]
+    weights = [
+        wall[:, :, at : at + width].reshape(width, width) for at in range(0, 3 * width, width)
+    ]
     wide = stream_ref[...].astype(jnp.float32) + contract_with(context[...], weights[0])
     attended = jnp.where(valid, wide, 0.0).astype(jnp.bfloat16)
     attended_ref[...] = attended
@@ -555,9 +563,8 @@
     for owner in received:
         twin_copy(call, owner).wait_send()
     relay.finish_sends(call)
-    relay.finish_sends(2)
     for owner in relay.column(me) + relay.column(relay.y_peer):
-        relay.copy(wall.at[1 - call, owner], 1 - call, owner, across, relay.c_peer).wait_send()
+        relay.copy(weight_slot(1 - call, owner), 1 - call, owner, across, relay.c_peer).wait_send()
     frames.finish_sends(0)
 
 
@@ -576,13 +583,13 @@
         ((1, count, rows, width), deep), ((count, depth, 3 * HEAD_DIM), deep),
         ((total, HEAD_DIM), deep), ((total + LEFT, HEAD_DIM), deep),
         ((total + LEFT, HEAD_DIM), deep),
-        ((3, depth, width), deep), ((3, count, depth, width), deep),
+        ((depth, 3 * width), deep), ((count, depth, 3 * width), deep),
         ((count, rows, HEAD_DIM), deep), ((count, rows, HEAD_DIM), deep),
         (stream.shape, deep), (stream.shape, deep), ((EDGE, width), deep), ((EDGE, width), deep),
         ((rows + 2 * EDGE, width), wide), ((rows, width), wide), ((2, width), wide),
         ((2, width), wide), ((7, 2, width), wide), ((planes - 1, 2, width), wide),
     ]
-    counts = [(count,)] * 3, [(count,)] * 3, [2, 2, 7, 7, planes - 1, planes - 1, 3, 10]
+    counts = [(count,)] * 3, [(count,)] * 3, [2, 2, 7, 7, planes - 1, planes - 1, 3, 9]
     sems = pltpu.SemaphoreType.DMA
     return pl.pallas_call(
         functools.partial(layer_kernel, count, HEAD_DIM**-0.5),
@@ -592,7 +599,7 @@
         scratch_shapes=[pltpu.VMEM(shape, kind) for shape, kind in buffers]
         + relay_sems(1, count)
         + [sems(shape) for shape in counts[0]]
-        + relay_sems(3, count)
+        + relay_sems(2, count)
         + [sems(shape) for shape in counts[1]]
         + [sems((size,)) for size in counts[2]],
         compiler_params=pltpu.CompilerParams(

time: 101 us -> 104 us (1.030)
  Pallas kernels: 91.7 us -> 95 us
    pallas_call x1, Pallas kernels: 91.7 us -> 95 us  [layer_call(): pl.pallas_call(functools.partial(layer_kernel, count, HEAD_DIM ** (-0.5))...]
where the time goes in v5:
time: 104 us
  Pallas kernels  95 us (91%)
  local copies, waits for them, and re-layouts  8.1 us (8%)
    pallas_call x1, Pallas kernels, layer_call(): pl.pallas_call(functools.partial(layer_kernel, count, HEAD_DIM ** (-0.5))...  95 us
    unnamed x22, local copies, waits for them, and re-layouts  8.1 us

profile of v5, /device:TPU:0, one launch (start us, length us, event | category | flops | bytes accessed | tf_op | source)
XLA Modules:
  0.0 103.7 jit_solution(15820896956468712063)
XLA Ops:
  0.6 0.0 copy-start.6
  0.6 0.0 copy-start.5
  0.7 0.0 copy-start.9
  0.7 0.7 copy-done.6
  1.3 0.0 copy-done.5
  1.3 0.0 copy-done.9
  1.3 0.0 copy-start
  1.3 1.0 copy-done
  2.3 0.0 copy-start.1
  2.3 0.9 copy-done.1
  3.3 0.0 copy-start.2
  3.3 0.9 copy-done.2
  4.2 0.0 copy-start.3
  4.2 0.9 copy-done.3
  5.1 0.0 copy-start.4
  5.1 0.8 copy-done.4
  6.0 0.0 copy-start.7
  6.0 0.7 copy-done.7
  6.7 0.0 copy-start.8
  6.7 0.7 copy-done.8
  7.4 95.0 %layer.1 = (bf16[128,1024]{1,0:T(8,128)(2,1)S(1)}, bf16[128,1024]{1,0:T(8,128)(2,1)S(1)}) custom-call(s32[2]{0:T(128)S(1)} %copy-done.9, bf16[128,1024]{1,0:T(8,128)(2,1)S(1)} %bitcast.9, f32[1,1024]{1,0:T(1,128)S(1)} %bitcast.10, bf16[64,3072]{1,0:T(8,128)(2,1)S(1)} %copy-done, bf16[64,1024]{1,0:T(8,128)(2,1)S(1)} %copy-done.3, f32[1,1024]{1,0:T(1,128)S(1)} %bitcast.11, ...), custom_call_target="tpu_custom_call" | custom-call | tf_op jit(solution)/shard_map/layer/pallas_call | solution.py:594
  102.3 0.7 copy.14
  103.0 0.7 copy.15
Async XLA Ops:
  0.6 0.7 copy-start.6
  0.6 0.7 copy-start.5
  0.7 0.7 copy-start.9
  1.3 1.0 copy-start
  2.3 0.9 copy-start.1
  3.3 0.9 copy-start.2
  4.2 0.9 copy-start.3
  5.1 0.8 copy-start.4
  6.0 0.7 copy-start.7
  6.7 0.7 copy-start.8

commit v6 on v4

--- a/solution.py
+++ b/solution.py
@@ -332,9 +332,17 @@
         pl.semaphore_signal(barrier, inc=1, device_id=where, device_id_type=MESH)
     k_ref[0:LEFT, :] = jnp.zeros((LEFT, HEAD_DIM), jnp.bfloat16)
     v_ref[0:LEFT, :] = jnp.zeros((LEFT, HEAD_DIM), jnp.bfloat16)
-    for get in gets:
+    gets[0].wait()
+    gets[1].wait()
+    x_ref[...] = layer_norm(stream_ref[...], gain1_ref[...]).astype(jnp.bfloat16)
+    own_x = pltpu.make_async_copy(x_ref, xall.at[0, me], own_sem.at[0])
+    own_w = pltpu.make_async_copy(w_ref.at[me], wcol.at[me], own_sem.at[1])
+    own_x.start()
+    pl.semaphore_wait(barrier, len(places))
+    frames.start(x_ref, 0)
+    frames.start_across(x_ref, 0)
+    for get in gets[2:]:
         get.wait()
-    x_ref[...] = layer_norm(stream_ref[...], gain1_ref[...]).astype(jnp.bfloat16)
     width = rows_ref.shape[1] // 3
     for head in range(count):
         for part in range(3):
@@ -342,12 +350,7 @@
             w_ref[head, :, part * HEAD_DIM : (part + 1) * HEAD_DIM] = rows_ref[
                 :, start : start + HEAD_DIM
             ]
-    own_x = pltpu.make_async_copy(x_ref, xall.at[0, me], own_sem.at[0])
-    own_w = pltpu.make_async_copy(w_ref.at[me], wcol.at[me], own_sem.at[1])
-    own_x.start()
     own_w.start()
-    pl.semaphore_wait(barrier, len(places))
-    frames.start(x_ref, 0)
 
     def slice_to(place):
         return remote(
@@ -362,7 +365,6 @@
         for step in range(1, count):
             slice_to((me + step) % count).start()
 
-    frames.start_across(x_ref, 0)
     steps = count // 4 - 1
     frames.step(0, 0)
     frames.step_over(-1, 0)
@@ -405,15 +407,18 @@
     frames.receive_across(0)
     w_columns = wcol[...].reshape(-1, 3 * HEAD_DIM)
 
-    def project_block(block, carry):
-        first = pl.multiple_of(block * SPAN, SPAN)
-        packed = contract_with(xall[0, block], w_columns).astype(jnp.bfloat16)
-        q_ref[pl.ds(first, SPAN), :] = packed[:, :HEAD_DIM]
-        k_ref[pl.ds(first + LEFT, SPAN), :] = packed[:, HEAD_DIM : 2 * HEAD_DIM]
-        v_ref[pl.ds(first + LEFT, SPAN), :] = packed[:, 2 * HEAD_DIM :]
+    group = 4 * SPAN
+
+    def project_group(at, carry):
+        first = pl.multiple_of(at * group, group)
+        rows = xall[0, pl.ds(4 * at, 4)].reshape(group, columns)
+        packed = contract_with(rows, w_columns).astype(jnp.bfloat16)
+        q_ref[pl.ds(first, group), :] = packed[:, :HEAD_DIM]
+        k_ref[pl.ds(first + LEFT, group), :] = packed[:, HEAD_DIM : 2 * HEAD_DIM]
+        v_ref[pl.ds(first + LEFT, group), :] = packed[:, 2 * HEAD_DIM :]
         return carry
 
-    lax.fori_loop(0, count, project_block, 0)
+    lax.fori_loop(0, count // 4, project_group, 0)
 
     def twin_copy(part, owner):
         return remote(
@@ -439,7 +444,9 @@
         query_pos = block * SPAN + lax.broadcasted_iota(jnp.int32, (SPAN, width), 0)
         allowed = (key_pos >= 0) & ((key_pos < length) | (key_pos == query_pos))
         raised = jnp.where(allowed, jnp.exp(scores * scale), 0.0)
-        probs = (raised / jnp.sum(raised, axis=-1, keepdims=True)).astype(jnp.bfloat16)
+        total = jnp.sum(raised, axis=-1, keepdims=True)
+        shrink = jnp.where(total > 1.0, 2.0**-32, 1.0).astype(jnp.float32)
+        probs = (raised * shrink * (1.0 / (total * shrink))).astype(jnp.bfloat16)
         mixed = jnp.dot(probs, v_ref[pl.ds(first, width), :], preferred_element_type=jnp.float32)
         return mixed.astype(jnp.bfloat16)
 

time: 101 us -> 97.8 us (0.968)
  Pallas kernels: 91.7 us -> 88.6 us
    pallas_call x1, Pallas kernels: 91.7 us -> 88.6 us  [layer_call(): pl.pallas_call(functools.partial(layer_kernel, count, HEAD_DIM ** (-0.5))...]
where the time goes in v6:
time: 97.8 us; the launch traced here: 97.4 us
  Pallas kernels  88.6 us (91%)
  local copies, waits for them, and re-layouts  8.1 us (8%)
    pallas_call x1, Pallas kernels, layer_call(): pl.pallas_call(functools.partial(layer_kernel, count, HEAD_DIM ** (-0.5))...  88.6 us
    unnamed x22, local copies, waits for them, and re-layouts  8.1 us

profile of v6, /device:TPU:0, one launch (start us, length us, event | category | flops | bytes accessed | tf_op | source)
XLA Modules:
  0.0 97.4 jit_solution(12962555368172631708)
XLA Ops:
  0.6 0.0 copy-start.6
  0.6 0.0 copy-start.5
  0.7 0.0 copy-start.9
  0.7 0.7 copy-done.6
  1.3 0.0 copy-done.5
  1.3 0.0 copy-done.9
  1.3 0.0 copy-start
  1.3 1.0 %copy-done = bf16[64,3072]{1,0:T(8,128)(2,1)S(1)} copy-done((bf16[64,3072]{1,0:T(8,128)(2,1)S(1)}, bf16[64,3072]{1,0:T(8,128)(2,1)}, u32[]{:S(2)}) %copy-start) | copy-done | bytes 393240
  2.3 0.0 copy-start.1
  2.3 0.9 copy-done.1
  3.3 0.0 copy-start.2
  3.3 0.9 copy-done.2
  4.2 0.0 copy-start.3
  4.2 0.9 copy-done.3
  5.1 0.0 copy-start.4
  5.1 0.8 copy-done.4
  6.0 0.0 copy-start.7
  6.0 0.7 copy-done.7
  6.7 0.0 copy-start.8
  6.7 0.7 copy-done.8
  7.4 88.6 %layer.1 = (bf16[128,1024]{1,0:T(8,128)(2,1)S(1)}, bf16[128,1024]{1,0:T(8,128)(2,1)S(1)}) custom-call(s32[2]{0:T(128)S(1)} %copy-done.9, bf16[128,1024]{1,0:T(8,128)(2,1)S(1)} %bitcast.9, f32[1,1024]{1,0:T(1,128)S(1)} %bitcast.10, bf16[64,3072]{1,0:T(8,128)(2,1)S(1)} %copy-done, bf16[64,1024]{1,0:T(8,128)(2,1)S(1)} %copy-done.3, f32[1,1024]{1,0:T(1,128)S(1)} %bitcast.11, ...), custom_call_target="tpu_custom_call" | custom-call | tf_op jit(solution)/shard_map/layer/pallas_call | solution.py:594
  96.0 0.7 copy.14
  96.7 0.7 copy.15
Async XLA Ops:
  0.6 0.7 copy-start.6
  0.6 0.7 copy-start.5
  0.7 0.7 copy-start.9
  1.3 1.0 %copy-start = (bf16[64,3072]{1,0:T(8,128)(2,1)S(1)}, bf16[64,3072]{1,0:T(8,128)(2,1)}, u32[]{:S(2)}) copy-start(bf16[64,3072]{1,0:T(8,128)(2,1)} %rows_any.1) | copy-start | bytes 1179652
  2.3 0.9 copy-start.1
  3.3 0.9 copy-start.2
  4.2 0.9 copy-start.3
  5.1 0.8 copy-start.4
  6.0 0.7 copy-start.7
  6.7 0.7 copy-start.8
